TPU v7x, 128 devices: a whole 4x4x4 slice. The times are simulated.
128 devices in a mesh: outer: 8 (over x_hi, y), inner: 16 (over z, x_lo, core).
Axes of the slice: x: 4 (x_hi: 2, x_lo: 2; x = x_hi * 2 + x_lo), y: 4, z: 4, core: 2. Of those that a mesh axis runs over, the one named last changes fastest.
Arguments:
- image_codes: int32 [24576, 768], P(('outer', 'inner')), may hold values from 32 to 207, as said below
- image_exps: int32 [24576, 6], P(('outer', 'inner')), may hold values from -8 to -4
- text_codes: int32 [24576, 768], P(('outer', 'inner')), may hold values from 32 to 207, as said below
- text_exps: int32 [24576, 6], P(('outer', 'inner')), may hold values from -8 to -4
- logit_scale: float32 [1], replicated, may hold values from 20 to 100
Outputs:
- mean_loss: float32 [], replicated
- image_grad: float32 [24576, 768], P(('outer', 'inner'))
- text_grad: float32 [24576, 768], P(('outer', 'inner'))
Inputs may be any that keep to these rules, and one draw needn't show every extreme that they name: `image_codes`: each code is an e4m3 byte: sign in bit 7, exponent field in bits 3 to 6, mantissa in bits 0 to 2; the exponent field is never 0 or 15. `text_codes`: each code is an e4m3 byte: sign in bit 7, exponent field in bits 3 to 6, mantissa in bits 0 to 2; the exponent field is never 0 or 15.
All inputs are finite; a program needn't handle non-finite values.
Results may differ from a plain program's by a relative error of at most 0.002.
Values may be sent and summed in bfloat16 or wider, within the bound.
A program may use at most 128 MiB of HBM per device.

v0:
```python
import jax
import jax.numpy as jnp
from jax import lax
from jax.sharding import PartitionSpec as P

MANT_UNIT = 2.0 ** (-9)


def as_sent(value):

    def short(part):
        return part.astype(jnp.bfloat16) if part.dtype == jnp.float32 else part

    return jax.tree.map(short, value)


def shifted_2(value, axis, by):
    peers = lax.axis_size(axis)
    return lax.ppermute(value, axis, [(i, (i + by) % peers) for i in range(peers)])


def merged_2(part, axis, combine):
    gathered = jax.tree.map(lambda a: lax.all_gather(a, axis), part)

    def take(source):
        return jax.tree.map(lambda a: lax.dynamic_index_in_dim(a, source, 0, False), gathered)

    return lax.fori_loop(
        1, lax.axis_size(axis), lambda source, state: combine(state, take(source)), take(0)
    )


def decode(code_values, exponents):
    sign_bit = code_values // 128
    exp_field = code_values // 8 % 16
    mantissa = code_values % 8
    significand = jnp.where(exp_field > 0, mantissa + 8, mantissa)
    power_int = jnp.left_shift(jnp.int32(1), jnp.maximum(exp_field, 1) - 1)
    magnitude = (significand * power_int).astype(jnp.float32) * MANT_UNIT
    signed_value = jnp.where(sign_bit > 0, -magnitude, magnitude)
    divisor = jnp.left_shift(jnp.int32(1), -exponents).astype(jnp.float32)
    row_count, feature_count = code_values.shape
    blocks = exponents.shape[1]
    shaped = signed_value.reshape(row_count, blocks, feature_count // blocks) / divisor[:, :, None]
    return shaped.reshape(row_count, feature_count).astype(jnp.bfloat16)


def score_tile(text_block, image_block, logit_mult):
    return logit_mult * lax.dot_general(
        text_block, image_block, (((1,), (1,)), ((), ())), preferred_element_type=jnp.float32
    )


def merge_lse(first, second):
    highest = jnp.maximum(first[0], second[0])
    return (
        highest,
        first[1] * jnp.exp(first[0] - highest) + second[1] * jnp.exp(second[0] - highest),
    )


def per_device(image_codes, image_exps, text_codes, text_exps, logit_scale):
    images = decode(image_codes, image_exps)
    text_rows = decode(text_codes, text_exps)
    logit_mult = logit_scale[0]
    rows_here = images.shape[0]
    feature_count = images.shape[1]
    cycle_size = lax.axis_size("outer")
    inner_size = lax.axis_size("inner")
    inner_pos = lax.axis_index("inner")
    text_group = lax.all_gather(text_rows, "inner", axis=0, tiled=True)
    group_rows = text_group.shape[0]

    def first_visit(pass_state):
        score_block = score_tile(text_group, pass_state["image_block"], logit_mult)
        highest_col = jnp.maximum(pass_state["col_max"], jnp.max(score_block, axis=1))
        col_sum = pass_state["col_sum"] * jnp.exp(pass_state["col_max"] - highest_col) + jnp.sum(
            jnp.exp(score_block - highest_col[:, None]), axis=1
        )
        tile_row = jnp.max(score_block, axis=0)
        row_part = jnp.sum(jnp.exp(score_block - tile_row[None, :]), axis=0)
        pass_state = dict(pass_state, col_max=highest_col, col_sum=col_sum)
        merged = merge_lse((pass_state["row_max"], pass_state["row_sum"]), (tile_row, row_part))
        pass_state = dict(pass_state, row_max=merged[0], row_sum=merged[1])
        return pass_state

    def first_move(pass_state):
        pass_state = dict(
            pass_state, image_block=shifted_2(as_sent(pass_state["image_block"]), "outer", 1)
        )
        shifted = shifted_2((pass_state["row_max"], pass_state["row_sum"]), "outer", 1)
        pass_state = dict(pass_state, row_max=shifted[0], row_sum=shifted[1])
        return pass_state

    pass_state = {
        "image_block": images,
        "col_max": jnp.full((group_rows,), -jnp.inf, jnp.float32),
        "col_sum": jnp.zeros((group_rows,), jnp.float32),
    }
    pass_state = dict(
        pass_state,
        row_max=jnp.full((rows_here,), -jnp.inf, jnp.float32),
        row_sum=jnp.zeros((rows_here,), jnp.float32),
    )
    pass_state = lax.fori_loop(
        0, cycle_size - 1, lambda cycle_step, current: first_move(first_visit(current)), pass_state
    )
    pass_state = first_visit(pass_state)
    home_max, home_sum = shifted_2((pass_state["row_max"], pass_state["row_sum"]), "outer", 1)
    row_lse = home_max + jnp.log(home_sum)
    col_highest, col_total = merged_2(
        (pass_state["col_max"], pass_state["col_sum"]), "inner", merge_lse
    )
    col_lse = col_highest + jnp.log(col_total)
    own_col = lax.dynamic_slice_in_dim(col_lse, inner_pos * rows_here, rows_here)
    image_wide = images.astype(jnp.float32)
    text_wide = text_rows.astype(jnp.float32)
    diagonal = logit_mult * jnp.sum(image_wide * text_wide, axis=1)
    loss_total = lax.psum(jnp.sum(row_lse + own_col - 2.0 * diagonal), ("outer", "inner"))
    mean_loss = loss_total / (2 * rows_here * cycle_size * inner_size)

    def grad_terms(image_block, block_lse):
        score_block = score_tile(text_group, image_block, logit_mult)
        weights = (
            (jnp.exp(score_block - col_lse[:, None]) + jnp.exp(score_block - block_lse[None, :]))
            * 0.5
        ).astype(jnp.bfloat16)
        text_term = jnp.dot(weights, image_block, preferred_element_type=jnp.float32)
        image_term = lax.dot_general(
            weights, text_group, (((0,), (0,)), ((), ())), preferred_element_type=jnp.float32
        )
        return (text_term, image_term)

    text_start = jnp.zeros((group_rows, feature_count), jnp.float32)

    def second_visit(cycle_carry):
        image_block, block_lse, block_grad, text_acc = cycle_carry
        text_term, image_term = grad_terms(image_block, block_lse)
        return (image_block, block_lse, block_grad + image_term, text_acc + text_term)

    def second_step(cycle_step, cycle_carry):
        image_block, block_lse, block_grad, text_acc = second_visit(cycle_carry)
        image_block = shifted_2(image_block, "outer", 1)
        block_lse, block_grad = shifted_2((block_lse, block_grad), "outer", 1)
        return (image_block, block_lse, block_grad, text_acc)

    cycle_carry = (images, row_lse, jnp.zeros((rows_here, feature_count), jnp.float32), text_start)
    cycle_carry = lax.fori_loop(0, cycle_size - 1, second_step, cycle_carry)
    cycle_carry = second_visit(cycle_carry)
    image_sums = shifted_2(cycle_carry[2], "outer", 1)
    text_acc = cycle_carry[3]
    text_sums = lax.psum_scatter(text_acc, "inner", scatter_dimension=0, tiled=True)
    image_grad = logit_mult * (image_sums - text_wide)
    text_grad = logit_mult * (text_sums - image_wide)
    return (mean_loss, image_grad, text_grad)


def solution(mesh):
    in_specs = (
        P(("outer", "inner"), None),
        P(("outer", "inner"), None),
        P(("outer", "inner"), None),
        P(("outer", "inner"), None),
        P(),
    )
    out_specs = (P(), P(("outer", "inner"), None), P(("outer", "inner"), None))
    return jax.shard_map(
        per_device, mesh=mesh, in_specs=in_specs, out_specs=out_specs, check_vma=False
    )
```

profile of v0, /device:TPU:1, one launch (start us, length us, event | category | flops | bytes accessed | tf_op | source)
XLA Modules:
  0.0 517.9 jit_solution(16118740006045790329)
XLA Ops:
  9.5 3.8 fusion.2
  14.2 41.6 %all-gather.4.cloned.1.call-done = bf16[3072,768]{1,0:T(8,128)(2,1)} async-done(((bf16[192,768]{1,0:T(8,128)(2,1)}), bf16[3072,768]{1,0:T(8,128)(2,1)}) %all-gather.4.cloned.1.call-update) | async-done | bytes 4718608 | tf_op jit(solution)/shard_map/all_gather | solution.py:71
  56.9 103.0 %while.54 = (s32[]{:T(128)}, f32[3072]{0:T(1024)S(1)}, f32[3072]{0:T(1024)}, bf16[192,768]{1,0:T(8,128)(2,1)S(1)}, f32[192]{0:T(256)}, /*index=5*/f32[192]{0:T(2...) while((s32[]{:T(128)}, f32[3072]{0:T(1024)S(1)}, f32[3072]{0:T(1024)}, ...), condition=%wide.region_5.6_spmd.clone, body=%wide.region_0.5_spmd.clone.sunk | while | flops 910114560 | bytes 11785364 | solution.py:105
  58.2 5.4 %fusion.58 = (f32[192]{0:T(256)S(1)}, f32[3072]{0:T(1024)}, f32[3072,192]{0,1:T(8,128)S(1)}) fusion(bf16[3072,768]{1,0:T(8,128)(2,1)} %get-tuple-element.535, bf16[192,768]{1,0:T(8,128)(2,1)S(1)} %copy.33, f32[]{:T(128)} %get-tuple-element.534), kind=kOutput, calls=%fused_computation.80.clone.1 | convolution fusion | flops 907735872 | bytes 7385860 | tf_op jit(solution)/shard_map/while/body/eval_jaxpr/dot_general | solution.py:49
  73.2 5.4 %fusion.58 = (f32[192]{0:T(256)S(1)}, f32[3072]{0:T(1024)}, f32[3072,192]{0,1:T(8,128)S(1)}) fusion(bf16[3072,768]{1,0:T(8,128)(2,1)} %get-tuple-element.535, bf16[192,768]{1,0:T(8,128)(2,1)S(1)} %copy.33, f32[]{:T(128)} %get-tuple-element.534), kind=kOutput, calls=%fused_computation.80.clone.1 | convolution fusion | flops 907735872 | bytes 7385860 | tf_op jit(solution)/shard_map/while/body/eval_jaxpr/dot_general | solution.py:49
  81.7 4.6 collective-permute-done.1
  87.3 5.4 %fusion.58 = (f32[192]{0:T(256)S(1)}, f32[3072]{0:T(1024)}, f32[3072,192]{0,1:T(8,128)S(1)}) fusion(bf16[3072,768]{1,0:T(8,128)(2,1)} %get-tuple-element.535, bf16[192,768]{1,0:T(8,128)(2,1)S(1)} %copy.33, f32[]{:T(128)} %get-tuple-element.534), kind=kOutput, calls=%fused_computation.80.clone.1 | convolution fusion | flops 907735872 | bytes 7385860 | tf_op jit(solution)/shard_map/while/body/eval_jaxpr/dot_general | solution.py:49
  96.6 3.6 collective-permute-done.1
  102.7 5.4 %fusion.58 = (f32[192]{0:T(256)S(1)}, f32[3072]{0:T(1024)}, f32[3072,192]{0,1:T(8,128)S(1)}) fusion(bf16[3072,768]{1,0:T(8,128)(2,1)} %get-tuple-element.535, bf16[192,768]{1,0:T(8,128)(2,1)S(1)} %copy.33, f32[]{:T(128)} %get-tuple-element.534), kind=kOutput, calls=%fused_computation.80.clone.1 | convolution fusion | flops 907735872 | bytes 7385860 | tf_op jit(solution)/shard_map/while/body/eval_jaxpr/dot_general | solution.py:49
  110.4 5.6 %collective-permute-done.1 = f32[192]{0:T(256)S(1)} collective-permute-done((f32[192]{0:T(256)S(1)}, f32[192]{0:T(256)S(1)}, u32[]{:S(2)}, u32[]{:S(2)}) %collective-permute-start.1) | collective-permute-done | bytes 800 | tf_op jit(solution)/shard_map/while/body/eval_jaxpr/ppermute | solution.py:19
  116.8 5.4 %fusion.58 = (f32[192]{0:T(256)S(1)}, f32[3072]{0:T(1024)}, f32[3072,192]{0,1:T(8,128)S(1)}) fusion(bf16[3072,768]{1,0:T(8,128)(2,1)} %get-tuple-element.535, bf16[192,768]{1,0:T(8,128)(2,1)S(1)} %copy.33, f32[]{:T(128)} %get-tuple-element.534), kind=kOutput, calls=%fused_computation.80.clone.1 | convolution fusion | flops 907735872 | bytes 7385860 | tf_op jit(solution)/shard_map/while/body/eval_jaxpr/dot_general | solution.py:49
  124.5 5.6 %collective-permute-done.1 = f32[192]{0:T(256)S(1)} collective-permute-done((f32[192]{0:T(256)S(1)}, f32[192]{0:T(256)S(1)}, u32[]{:S(2)}, u32[]{:S(2)}) %collective-permute-start.1) | collective-permute-done | bytes 800 | tf_op jit(solution)/shard_map/while/body/eval_jaxpr/ppermute | solution.py:19
  130.9 5.4 %fusion.58 = (f32[192]{0:T(256)S(1)}, f32[3072]{0:T(1024)}, f32[3072,192]{0,1:T(8,128)S(1)}) fusion(bf16[3072,768]{1,0:T(8,128)(2,1)} %get-tuple-element.535, bf16[192,768]{1,0:T(8,128)(2,1)S(1)} %copy.33, f32[]{:T(128)} %get-tuple-element.534), kind=kOutput, calls=%fused_computation.80.clone.1 | convolution fusion | flops 907735872 | bytes 7385860 | tf_op jit(solution)/shard_map/while/body/eval_jaxpr/dot_general | solution.py:49
  138.6 5.3 %collective-permute-done.1 = f32[192]{0:T(256)S(1)} collective-permute-done((f32[192]{0:T(256)S(1)}, f32[192]{0:T(256)S(1)}, u32[]{:S(2)}, u32[]{:S(2)}) %collective-permute-start.1) | collective-permute-done | bytes 800 | tf_op jit(solution)/shard_map/while/body/eval_jaxpr/ppermute | solution.py:19
  144.7 5.4 %fusion.58 = (f32[192]{0:T(256)S(1)}, f32[3072]{0:T(1024)}, f32[3072,192]{0,1:T(8,128)S(1)}) fusion(bf16[3072,768]{1,0:T(8,128)(2,1)} %get-tuple-element.535, bf16[192,768]{1,0:T(8,128)(2,1)S(1)} %copy.33, f32[]{:T(128)} %get-tuple-element.534), kind=kOutput, calls=%fused_computation.80.clone.1 | convolution fusion | flops 907735872 | bytes 7385860 | tf_op jit(solution)/shard_map/while/body/eval_jaxpr/dot_general | solution.py:49
  154.0 3.7 collective-permute-done.1
  159.9 4.1 fusion.25
  164.9 29.7 %all-gather.1 = f32[49152]{0:T(1024)S(1)} all-gather(f32[3072]{0:T(1024)S(1)} %multiply_add_fusion.2), channel_id=3, replica_groups=mesh['outer'=8,'inner'=16] {'inner'}, dimensions={0}, use_global_device_ids=true | all-gather | bytes 208896 | tf_op jit(solution)/shard_map/all_gather | solution.py:23
  194.6 17.4 %all-gather = f32[49152]{0:T(1024)S(1)} all-gather(f32[3072]{0:T(1024)S(1)} %max.31), channel_id=2, replica_groups=mesh['outer'=8,'inner'=16] {'inner'}, dimensions={0}, use_global_device_ids=true | all-gather | bytes 208896 | tf_op jit(solution)/shard_map/all_gather | solution.py:23
  213.6 4.6 collective-permute-done.6
  219.2 160.2 %while.55 = (s32[]{:T(128)}, bf16[192,768]{1,0:T(8,128)(2,1)S(1)}, f32[192]{0:T(256)S(1)}, f32[192,768]{1,0:T(8,128)S(1)}, f32[3072,768]{1,0:T(8,128)}, /*index=...) while((s32[]{:T(128)}, bf16[192,768]{1,0:T(8,128)(2,1)S(1)}, ...), condition=%wide.region_16.17_spmd.clone, body=%wide.region_15.16_spmd.clone.sunk | while | flops 2726313984 | bytes 51922456 | solution.py:148
  219.4 5.3 %multiply_convert_fusion.3 = bf16[3072,192]{0,1:T(8,128)(2,1)S(1)} fusion(bf16[3072,768]{1,0:T(8,128)(2,1)} %get-tuple-element.588, bf16[192,768]{1,0:T(8,128)(2,1)S(1)} %copy.57, f32[192]{0:T(256)S(1)} %copy.58, f32[3072]{0:T(1024)S(1)} %get-tuple-element.589, f32[]{:T(128)} %get-tuple-element.587), kind=kOutput, calls=%fused_computation.12.clone.1 | convolution fusion | flops 909508608 | bytes 6206212 | tf_op jit(solution)/shard_map/while/body/eval_jaxpr/dot_general | solution.py:49
  226.2 5.1 select_add_fusion.2
  231.3 11.8 %collective-permute-done.5 = f32[192,768]{1,0:T(8,128)S(1)} collective-permute-done((f32[192,768]{1,0:T(8,128)S(1)}, f32[192,768]{1,0:T(8,128)S(1)}, u32[]{:S(2)}, u32[]{:S(2)}) %collective-permute-start.5) | collective-permute-done | bytes 589856 | tf_op jit(solution)/shard_map/while/body/eval_jaxpr/ppermute | solution.py:19
  243.4 5.4 %multiply_convert_fusion.3 = bf16[3072,192]{0,1:T(8,128)(2,1)S(1)} fusion(bf16[3072,768]{1,0:T(8,128)(2,1)} %get-tuple-element.588, bf16[192,768]{1,0:T(8,128)(2,1)S(1)} %copy.57, f32[192]{0:T(256)S(1)} %copy.58, f32[3072]{0:T(1024)S(1)} %get-tuple-element.589, f32[]{:T(128)} %get-tuple-element.587), kind=kOutput, calls=%fused_computation.12.clone.1 | convolution fusion | flops 909508608 | bytes 6206212 | tf_op jit(solution)/shard_map/while/body/eval_jaxpr/dot_general | solution.py:49
  250.0 8.8 %select_add_fusion.2 = f32[3072,768]{1,0:T(8,128)} fusion(f32[3072,768]{1,0:T(8,128)} %get-tuple-element.576, bf16[3072,192]{0,1:T(8,128)(2,1)S(1)} %multiply_convert_fusion.3, bf16[192,768]{1,0:T(8,128)(2,1)S(1)} %copy.57, pred[]{:T(512)S(6)} %compare.19), kind=kOutput, calls=%fused_computation.10.clone.1 | convolution fusion | flops 910688256 | bytes 20348928 | tf_op jit(solution)/shard_map/while/body/eval_jaxpr/dot_general | solution.py:128
  258.8 6.9 %collective-permute-done.5 = f32[192,768]{1,0:T(8,128)S(1)} collective-permute-done((f32[192,768]{1,0:T(8,128)S(1)}, f32[192,768]{1,0:T(8,128)S(1)}, u32[]{:S(2)}, u32[]{:S(2)}) %collective-permute-start.5) | collective-permute-done | bytes 589856 | tf_op jit(solution)/shard_map/while/body/eval_jaxpr/ppermute | solution.py:19
  266.1 5.2 multiply_convert_fusion.3
  272.6 8.8 %select_add_fusion.2 = f32[3072,768]{1,0:T(8,128)} fusion(f32[3072,768]{1,0:T(8,128)} %get-tuple-element.576, bf16[3072,192]{0,1:T(8,128)(2,1)S(1)} %multiply_convert_fusion.3, bf16[192,768]{1,0:T(8,128)(2,1)S(1)} %copy.57, pred[]{:T(512)S(6)} %compare.19), kind=kOutput, calls=%fused_computation.10.clone.1 | convolution fusion | flops 910688256 | bytes 20348928 | tf_op jit(solution)/shard_map/while/body/eval_jaxpr/dot_general | solution.py:128
  281.4 6.2 %collective-permute-done.5 = f32[192,768]{1,0:T(8,128)S(1)} collective-permute-done((f32[192,768]{1,0:T(8,128)S(1)}, f32[192,768]{1,0:T(8,128)S(1)}, u32[]{:S(2)}, u32[]{:S(2)}) %collective-permute-start.5) | collective-permute-done | bytes 589856 | tf_op jit(solution)/shard_map/while/body/eval_jaxpr/ppermute | solution.py:19
  287.8 5.4 %multiply_convert_fusion.3 = bf16[3072,192]{0,1:T(8,128)(2,1)S(1)} fusion(bf16[3072,768]{1,0:T(8,128)(2,1)} %get-tuple-element.588, bf16[192,768]{1,0:T(8,128)(2,1)S(1)} %copy.57, f32[192]{0:T(256)S(1)} %copy.58, f32[3072]{0:T(1024)S(1)} %get-tuple-element.589, f32[]{:T(128)} %get-tuple-element.587), kind=kOutput, calls=%fused_computation.12.clone.1 | convolution fusion | flops 909508608 | bytes 6206212 | tf_op jit(solution)/shard_map/while/body/eval_jaxpr/dot_general | solution.py:49
  294.4 8.8 %select_add_fusion.2 = f32[3072,768]{1,0:T(8,128)} fusion(f32[3072,768]{1,0:T(8,128)} %get-tuple-element.576, bf16[3072,192]{0,1:T(8,128)(2,1)S(1)} %multiply_convert_fusion.3, bf16[192,768]{1,0:T(8,128)(2,1)S(1)} %copy.57, pred[]{:T(512)S(6)} %compare.19), kind=kOutput, calls=%fused_computation.10.clone.1 | convolution fusion | flops 910688256 | bytes 20348928 | tf_op jit(solution)/shard_map/while/body/eval_jaxpr/dot_general | solution.py:128
  303.2 6.6 %collective-permute-done.5 = f32[192,768]{1,0:T(8,128)S(1)} collective-permute-done((f32[192,768]{1,0:T(8,128)S(1)}, f32[192,768]{1,0:T(8,128)S(1)}, u32[]{:S(2)}, u32[]{:S(2)}) %collective-permute-start.5) | collective-permute-done | bytes 589856 | tf_op jit(solution)/shard_map/while/body/eval_jaxpr/ppermute | solution.py:19
  310.0 5.4 %multiply_convert_fusion.3 = bf16[3072,192]{0,1:T(8,128)(2,1)S(1)} fusion(bf16[3072,768]{1,0:T(8,128)(2,1)} %get-tuple-element.588, bf16[192,768]{1,0:T(8,128)(2,1)S(1)} %copy.57, f32[192]{0:T(256)S(1)} %copy.58, f32[3072]{0:T(1024)S(1)} %get-tuple-element.589, f32[]{:T(128)} %get-tuple-element.587), kind=kOutput, calls=%fused_computation.12.clone.1 | convolution fusion | flops 909508608 | bytes 6206212 | tf_op jit(solution)/shard_map/while/body/eval_jaxpr/dot_general | solution.py:49
  316.7 8.8 %select_add_fusion.2 = f32[3072,768]{1,0:T(8,128)} fusion(f32[3072,768]{1,0:T(8,128)} %get-tuple-element.576, bf16[3072,192]{0,1:T(8,128)(2,1)S(1)} %multiply_convert_fusion.3, bf16[192,768]{1,0:T(8,128)(2,1)S(1)} %copy.57, pred[]{:T(512)S(6)} %compare.19), kind=kOutput, calls=%fused_computation.10.clone.1 | convolution fusion | flops 910688256 | bytes 20348928 | tf_op jit(solution)/shard_map/while/body/eval_jaxpr/dot_general | solution.py:128
  325.4 7.5 %collective-permute-done.5 = f32[192,768]{1,0:T(8,128)S(1)} collective-permute-done((f32[192,768]{1,0:T(8,128)S(1)}, f32[192,768]{1,0:T(8,128)S(1)}, u32[]{:S(2)}, u32[]{:S(2)}) %collective-permute-start.5) | collective-permute-done | bytes 589856 | tf_op jit(solution)/shard_map/while/body/eval_jaxpr/ppermute | solution.py:19
  333.1 5.4 %multiply_convert_fusion.3 = bf16[3072,192]{0,1:T(8,128)(2,1)S(1)} fusion(bf16[3072,768]{1,0:T(8,128)(2,1)} %get-tuple-element.588, bf16[192,768]{1,0:T(8,128)(2,1)S(1)} %copy.57, f32[192]{0:T(256)S(1)} %copy.58, f32[3072]{0:T(1024)S(1)} %get-tuple-element.589, f32[]{:T(128)} %get-tuple-element.587), kind=kOutput, calls=%fused_computation.12.clone.1 | convolution fusion | flops 909508608 | bytes 6206212 | tf_op jit(solution)/shard_map/while/body/eval_jaxpr/dot_general | solution.py:49
  339.8 8.8 %select_add_fusion.2 = f32[3072,768]{1,0:T(8,128)} fusion(f32[3072,768]{1,0:T(8,128)} %get-tuple-element.576, bf16[3072,192]{0,1:T(8,128)(2,1)S(1)} %multiply_convert_fusion.3, bf16[192,768]{1,0:T(8,128)(2,1)S(1)} %copy.57, pred[]{:T(512)S(6)} %compare.19), kind=kOutput, calls=%fused_computation.10.clone.1 | convolution fusion | flops 910688256 | bytes 20348928 | tf_op jit(solution)/shard_map/while/body/eval_jaxpr/dot_general | solution.py:128
  348.5 7.8 %collective-permute-done.5 = f32[192,768]{1,0:T(8,128)S(1)} collective-permute-done((f32[192,768]{1,0:T(8,128)S(1)}, f32[192,768]{1,0:T(8,128)S(1)}, u32[]{:S(2)}, u32[]{:S(2)}) %collective-permute-start.5) | collective-permute-done | bytes 589856 | tf_op jit(solution)/shard_map/while/body/eval_jaxpr/ppermute | solution.py:19
  356.5 5.4 %multiply_convert_fusion.3 = bf16[3072,192]{0,1:T(8,128)(2,1)S(1)} fusion(bf16[3072,768]{1,0:T(8,128)(2,1)} %get-tuple-element.588, bf16[192,768]{1,0:T(8,128)(2,1)S(1)} %copy.57, f32[192]{0:T(256)S(1)} %copy.58, f32[3072]{0:T(1024)S(1)} %get-tuple-element.589, f32[]{:T(128)} %get-tuple-element.587), kind=kOutput, calls=%fused_computation.12.clone.1 | convolution fusion | flops 909508608 | bytes 6206212 | tf_op jit(solution)/shard_map/while/body/eval_jaxpr/dot_general | solution.py:49
  363.2 8.8 %select_add_fusion.2 = f32[3072,768]{1,0:T(8,128)} fusion(f32[3072,768]{1,0:T(8,128)} %get-tuple-element.576, bf16[3072,192]{0,1:T(8,128)(2,1)S(1)} %multiply_convert_fusion.3, bf16[192,768]{1,0:T(8,128)(2,1)S(1)} %copy.57, pred[]{:T(512)S(6)} %compare.19), kind=kOutput, calls=%fused_computation.10.clone.1 | convolution fusion | flops 910688256 | bytes 20348928 | tf_op jit(solution)/shard_map/while/body/eval_jaxpr/dot_general | solution.py:128
  372.0 7.5 %collective-permute-done.5 = f32[192,768]{1,0:T(8,128)S(1)} collective-permute-done((f32[192,768]{1,0:T(8,128)S(1)}, f32[192,768]{1,0:T(8,128)S(1)}, u32[]{:S(2)}, u32[]{:S(2)}) %collective-permute-start.5) | collective-permute-done | bytes 589856 | tf_op jit(solution)/shard_map/while/body/eval_jaxpr/ppermute | solution.py:19
  379.4 4.1 multiply_convert_fusion.1
  383.6 5.1 fusion.29
  388.7 11.2 %add.143 = f32[3072,768]{1,0:T(8,128)} add(f32[3072,768]{1,0:T(8,128)} %get-tuple-element.237, f32[3072,768]{1,0:T(8,128)} %fusion.29) | non-fusion elementwise | flops 2359296 | bytes 28311552 | tf_op jit(solution)/shard_map/add | solution.py:139
  399.9 3.5 fusion.28
  403.6 87.3 %psum.7 = f32[]{:T(128)} all-reduce(f32[]{:T(128)} %get-tuple-element.346), channel_id=1, replica_groups=mesh['outer'=8,'inner'=16] {'outer','inner'}, use_global_device_ids=true, to_apply=%region_14.15 | all-reduce | flops 1 | bytes 8 | tf_op jit(solution)/shard_map/psum | solution.py:119
  492.4 15.6 %reduce-scatter.2.cloned.1.call-done = f32[192,768]{1,0:T(8,128)} async-done(((f32[3072,768]{1,0:T(8,128)}), f32[192,768]{1,0:T(8,128)}) %reduce-scatter.2.cloned.1.call-update) | async-done | bytes 589840 | tf_op jit(solution)/shard_map/reduce_scatter | solution.py:152
  (334 shorter events, 57.6 us)
Async XLA Ops:
  7.2 48.6 %all-gather.4.cloned.1.call-start = ((), (), s32[]{:S(2)}) async-start(), calls=%async_computation.1 | async-start | bytes 5013504 | tf_op jit(solution)/shard_map/all_gather | solution.py:71
  13.4 494.6 %reduce-scatter.2.cloned.1.call-start = ((), (), s32[]{:S(2)}) async-start(), calls=%async_computation.2 | async-start | bytes 10027008 | tf_op jit(solution)/shard_map/reduce_scatter | solution.py:152
  57.0 15.6 %collective-permute-start = (bf16[192,768]{1,0:T(8,128)(2,1)S(1)}, bf16[192,768]{1,0:T(8,128)(2,1)S(1)}, u32[]{:S(2)}, u32[]{:S(2)}) collective-permute-start(bf16[192,768]{1,0:T(8,128)(2,1)S(1)} %copy.33), channel_id=1, source_target_pairs={{0,16},{16,32},{32,48},{48,64},{64,80},{80,96},{96,112},{112,0},{1... | collective-permute-start | bytes 884744 | tf_op jit(solution)/shard_map/while/body/eval_jaxpr/ppermute | solution.py:19
  65.1 6.1 %collective-permute-start.1 = (f32[192]{0:T(256)S(1)}, f32[192]{0:T(256)S(1)}, u32[]{:S(2)}, u32[]{:S(2)}) collective-permute-start(f32[192]{0:T(256)S(1)} %get-tuple-element.498), channel_id=1, source_target_pairs={{0,16},{16,32},{32,48},{48,64},{64,80},{80,96},{96,112},{112,0},{1... | collective-permute-start | bytes 2312 | tf_op jit(solution)/shard_map/while/body/eval_jaxpr/ppermute | solution.py:19
  66.4 6.1 %collective-permute-start.2 = (f32[192]{0:T(256)S(1)}, f32[192]{0:T(256)S(1)}, u32[]{:S(2)}, u32[]{:S(2)}) collective-permute-start(f32[192]{0:T(256)S(1)} %get-tuple-element.499), channel_id=1, source_target_pairs={{0,16},{16,32},{32,48},{48,64},{64,80},{80,96},{96,112},{112,0},{1... | collective-permute-start | bytes 2312 | tf_op jit(solution)/shard_map/while/body/eval_jaxpr/ppermute | solution.py:19
  73.2 13.2 %collective-permute-start = (bf16[192,768]{1,0:T(8,128)(2,1)S(1)}, bf16[192,768]{1,0:T(8,128)(2,1)S(1)}, u32[]{:S(2)}, u32[]{:S(2)}) collective-permute-start(bf16[192,768]{1,0:T(8,128)(2,1)S(1)} %copy.33), channel_id=1, source_target_pairs={{0,16},{16,32},{32,48},{48,64},{64,80},{80,96},{96,112},{112,0},{1... | collective-permute-start | bytes 884744 | tf_op jit(solution)/shard_map/while/body/eval_jaxpr/ppermute | solution.py:19
  80.2 6.1 %collective-permute-start.1 = (f32[192]{0:T(256)S(1)}, f32[192]{0:T(256)S(1)}, u32[]{:S(2)}, u32[]{:S(2)}) collective-permute-start(f32[192]{0:T(256)S(1)} %get-tuple-element.498), channel_id=1, source_target_pairs={{0,16},{16,32},{32,48},{48,64},{64,80},{80,96},{96,112},{112,0},{1... | collective-permute-start | bytes 2312 | tf_op jit(solution)/shard_map/while/body/eval_jaxpr/ppermute | solution.py:19
  80.2 6.1 %collective-permute-start.2 = (f32[192]{0:T(256)S(1)}, f32[192]{0:T(256)S(1)}, u32[]{:S(2)}, u32[]{:S(2)}) collective-permute-start(f32[192]{0:T(256)S(1)} %get-tuple-element.499), channel_id=1, source_target_pairs={{0,16},{16,32},{32,48},{48,64},{64,80},{80,96},{96,112},{112,0},{1... | collective-permute-start | bytes 2312 | tf_op jit(solution)/shard_map/while/body/eval_jaxpr/ppermute | solution.py:19
  86.9 15.0 %collective-permute-start = (bf16[192,768]{1,0:T(8,128)(2,1)S(1)}, bf16[192,768]{1,0:T(8,128)(2,1)S(1)}, u32[]{:S(2)}, u32[]{:S(2)}) collective-permute-start(bf16[192,768]{1,0:T(8,128)(2,1)S(1)} %copy.33), channel_id=1, source_target_pairs={{0,16},{16,32},{32,48},{48,64},{64,80},{80,96},{96,112},{112,0},{1... | collective-permute-start | bytes 884744 | tf_op jit(solution)/shard_map/while/body/eval_jaxpr/ppermute | solution.py:19
  94.2 6.1 %collective-permute-start.1 = (f32[192]{0:T(256)S(1)}, f32[192]{0:T(256)S(1)}, u32[]{:S(2)}, u32[]{:S(2)}) collective-permute-start(f32[192]{0:T(256)S(1)} %get-tuple-element.498), channel_id=1, source_target_pairs={{0,16},{16,32},{32,48},{48,64},{64,80},{80,96},{96,112},{112,0},{1... | collective-permute-start | bytes 2312 | tf_op jit(solution)/shard_map/while/body/eval_jaxpr/ppermute | solution.py:19
  95.9 6.0 %collective-permute-start.2 = (f32[192]{0:T(256)S(1)}, f32[192]{0:T(256)S(1)}, u32[]{:S(2)}, u32[]{:S(2)}) collective-permute-start(f32[192]{0:T(256)S(1)} %get-tuple-element.499), channel_id=1, source_target_pairs={{0,16},{16,32},{32,48},{48,64},{64,80},{80,96},{96,112},{112,0},{1... | collective-permute-start | bytes 2312 | tf_op jit(solution)/shard_map/while/body/eval_jaxpr/ppermute | solution.py:19
  102.6 13.5 %collective-permute-start = (bf16[192,768]{1,0:T(8,128)(2,1)S(1)}, bf16[192,768]{1,0:T(8,128)(2,1)S(1)}, u32[]{:S(2)}, u32[]{:S(2)}) collective-permute-start(bf16[192,768]{1,0:T(8,128)(2,1)S(1)} %copy.33), channel_id=1, source_target_pairs={{0,16},{16,32},{32,48},{48,64},{64,80},{80,96},{96,112},{112,0},{1... | collective-permute-start | bytes 884744 | tf_op jit(solution)/shard_map/while/body/eval_jaxpr/ppermute | solution.py:19
  109.6 6.4 %collective-permute-start.1 = (f32[192]{0:T(256)S(1)}, f32[192]{0:T(256)S(1)}, u32[]{:S(2)}, u32[]{:S(2)}) collective-permute-start(f32[192]{0:T(256)S(1)} %get-tuple-element.498), channel_id=1, source_target_pairs={{0,16},{16,32},{32,48},{48,64},{64,80},{80,96},{96,112},{112,0},{1... | collective-permute-start | bytes 2312 | tf_op jit(solution)/shard_map/while/body/eval_jaxpr/ppermute | solution.py:19
  109.7 6.4 %collective-permute-start.2 = (f32[192]{0:T(256)S(1)}, f32[192]{0:T(256)S(1)}, u32[]{:S(2)}, u32[]{:S(2)}) collective-permute-start(f32[192]{0:T(256)S(1)} %get-tuple-element.499), channel_id=1, source_target_pairs={{0,16},{16,32},{32,48},{48,64},{64,80},{80,96},{96,112},{112,0},{1... | collective-permute-start | bytes 2312 | tf_op jit(solution)/shard_map/while/body/eval_jaxpr/ppermute | solution.py:19
  116.7 13.5 %collective-permute-start = (bf16[192,768]{1,0:T(8,128)(2,1)S(1)}, bf16[192,768]{1,0:T(8,128)(2,1)S(1)}, u32[]{:S(2)}, u32[]{:S(2)}) collective-permute-start(bf16[192,768]{1,0:T(8,128)(2,1)S(1)} %copy.33), channel_id=1, source_target_pairs={{0,16},{16,32},{32,48},{48,64},{64,80},{80,96},{96,112},{112,0},{1... | collective-permute-start | bytes 884744 | tf_op jit(solution)/shard_map/while/body/eval_jaxpr/ppermute | solution.py:19
  123.7 6.4 %collective-permute-start.1 = (f32[192]{0:T(256)S(1)}, f32[192]{0:T(256)S(1)}, u32[]{:S(2)}, u32[]{:S(2)}) collective-permute-start(f32[192]{0:T(256)S(1)} %get-tuple-element.498), channel_id=1, source_target_pairs={{0,16},{16,32},{32,48},{48,64},{64,80},{80,96},{96,112},{112,0},{1... | collective-permute-start | bytes 2312 | tf_op jit(solution)/shard_map/while/body/eval_jaxpr/ppermute | solution.py:19
  123.8 6.4 %collective-permute-start.2 = (f32[192]{0:T(256)S(1)}, f32[192]{0:T(256)S(1)}, u32[]{:S(2)}, u32[]{:S(2)}) collective-permute-start(f32[192]{0:T(256)S(1)} %get-tuple-element.499), channel_id=1, source_target_pairs={{0,16},{16,32},{32,48},{48,64},{64,80},{80,96},{96,112},{112,0},{1... | collective-permute-start | bytes 2312 | tf_op jit(solution)/shard_map/while/body/eval_jaxpr/ppermute | solution.py:19
  130.8 13.2 %collective-permute-start = (bf16[192,768]{1,0:T(8,128)(2,1)S(1)}, bf16[192,768]{1,0:T(8,128)(2,1)S(1)}, u32[]{:S(2)}, u32[]{:S(2)}) collective-permute-start(bf16[192,768]{1,0:T(8,128)(2,1)S(1)} %copy.33), channel_id=1, source_target_pairs={{0,16},{16,32},{32,48},{48,64},{64,80},{80,96},{96,112},{112,0},{1... | collective-permute-start | bytes 884744 | tf_op jit(solution)/shard_map/while/body/eval_jaxpr/ppermute | solution.py:19
  137.8 6.1 %collective-permute-start.1 = (f32[192]{0:T(256)S(1)}, f32[192]{0:T(256)S(1)}, u32[]{:S(2)}, u32[]{:S(2)}) collective-permute-start(f32[192]{0:T(256)S(1)} %get-tuple-element.498), channel_id=1, source_target_pairs={{0,16},{16,32},{32,48},{48,64},{64,80},{80,96},{96,112},{112,0},{1... | collective-permute-start | bytes 2312 | tf_op jit(solution)/shard_map/while/body/eval_jaxpr/ppermute | solution.py:19
  137.9 6.1 %collective-permute-start.2 = (f32[192]{0:T(256)S(1)}, f32[192]{0:T(256)S(1)}, u32[]{:S(2)}, u32[]{:S(2)}) collective-permute-start(f32[192]{0:T(256)S(1)} %get-tuple-element.499), channel_id=1, source_target_pairs={{0,16},{16,32},{32,48},{48,64},{64,80},{80,96},{96,112},{112,0},{1... | collective-permute-start | bytes 2312 | tf_op jit(solution)/shard_map/while/body/eval_jaxpr/ppermute | solution.py:19
  144.6 14.8 %collective-permute-start = (bf16[192,768]{1,0:T(8,128)(2,1)S(1)}, bf16[192,768]{1,0:T(8,128)(2,1)S(1)}, u32[]{:S(2)}, u32[]{:S(2)}) collective-permute-start(bf16[192,768]{1,0:T(8,128)(2,1)S(1)} %copy.33), channel_id=1, source_target_pairs={{0,16},{16,32},{32,48},{48,64},{64,80},{80,96},{96,112},{112,0},{1... | collective-permute-start | bytes 884744 | tf_op jit(solution)/shard_map/while/body/eval_jaxpr/ppermute | solution.py:19
  151.6 6.1 %collective-permute-start.1 = (f32[192]{0:T(256)S(1)}, f32[192]{0:T(256)S(1)}, u32[]{:S(2)}, u32[]{:S(2)}) collective-permute-start(f32[192]{0:T(256)S(1)} %get-tuple-element.498), channel_id=1, source_target_pairs={{0,16},{16,32},{32,48},{48,64},{64,80},{80,96},{96,112},{112,0},{1... | collective-permute-start | bytes 2312 | tf_op jit(solution)/shard_map/while/body/eval_jaxpr/ppermute | solution.py:19
  153.3 6.0 %collective-permute-start.2 = (f32[192]{0:T(256)S(1)}, f32[192]{0:T(256)S(1)}, u32[]{:S(2)}, u32[]{:S(2)}) collective-permute-start(f32[192]{0:T(256)S(1)} %get-tuple-element.499), channel_id=1, source_target_pairs={{0,16},{16,32},{32,48},{48,64},{64,80},{80,96},{96,112},{112,0},{1... | collective-permute-start | bytes 2312 | tf_op jit(solution)/shard_map/while/body/eval_jaxpr/ppermute | solution.py:19
  212.1 6.1 %collective-permute-start.6 = (f32[192]{0:T(256)S(1)}, f32[192]{0:T(256)S(1)}, u32[]{:S(2)}, u32[]{:S(2)}) collective-permute-start(f32[192]{0:T(256)S(1)} %get-tuple-element.349), channel_id=1, source_target_pairs={{0,16},{16,32},{32,48},{48,64},{64,80},{80,96},{96,112},{112,0},{1... | collective-permute-start | bytes 2312 | tf_op jit(solution)/shard_map/ppermute | solution.py:19
  212.2 6.3 %collective-permute-start.7 = (f32[192]{0:T(256)S(1)}, f32[192]{0:T(256)S(1)}, u32[]{:S(2)}, u32[]{:S(2)}) collective-permute-start(f32[192]{0:T(256)S(1)} %get-tuple-element.348), channel_id=1, source_target_pairs={{0,16},{16,32},{32,48},{48,64},{64,80},{80,96},{96,112},{112,0},{1... | collective-permute-start | bytes 2312 | tf_op jit(solution)/shard_map/ppermute | solution.py:19
  219.2 12.1 %collective-permute-start.3 = (bf16[192,768]{1,0:T(8,128)(2,1)S(1)}, bf16[192,768]{1,0:T(8,128)(2,1)S(1)}, u32[]{:S(2)}, u32[]{:S(2)}) collective-permute-start(bf16[192,768]{1,0:T(8,128)(2,1)S(1)} %copy.57), channel_id=1, source_target_pairs={{0,16},{16,32},{32,48},{48,64},{64,80},{80,96},{96,112},{112,0},{1... | collective-permute-start | bytes 884744 | tf_op jit(solution)/shard_map/while/body/eval_jaxpr/ppermute | solution.py:19
  219.3 12.0 %collective-permute-start.4 = (f32[192]{0:T(256)S(1)}, f32[192]{0:T(256)S(1)}, u32[]{:S(2)}, u32[]{:S(2)}) collective-permute-start(f32[192]{0:T(256)S(1)} %copy.58), channel_id=1, source_target_pairs={{0,16},{16,32},{32,48},{48,64},{64,80},{80,96},{96,112},{112,0},{1... | collective-permute-start | bytes 2312 | tf_op jit(solution)/shard_map/while/body/eval_jaxpr/ppermute | solution.py:19
  226.0 17.2 %collective-permute-start.5 = (f32[192,768]{1,0:T(8,128)S(1)}, f32[192,768]{1,0:T(8,128)S(1)}, u32[]{:S(2)}, u32[]{:S(2)}) collective-permute-start(f32[192,768]{1,0:T(8,128)S(1)} %convolution_add_fusion.2), channel_id=1, source_target_pairs={{0,16},{16,32},{32,48},{48,64},{64,80},{80,96},{96,112},{112,0},{1... | collective-permute-start | bytes 1769480 | tf_op jit(solution)/shard_map/while/body/eval_jaxpr/ppermute | solution.py:19
  243.2 15.6 %collective-permute-start.3 = (bf16[192,768]{1,0:T(8,128)(2,1)S(1)}, bf16[192,768]{1,0:T(8,128)(2,1)S(1)}, u32[]{:S(2)}, u32[]{:S(2)}) collective-permute-start(bf16[192,768]{1,0:T(8,128)(2,1)S(1)} %copy.57), channel_id=1, source_target_pairs={{0,16},{16,32},{32,48},{48,64},{64,80},{80,96},{96,112},{112,0},{1... | collective-permute-start | bytes 884744 | tf_op jit(solution)/shard_map/while/body/eval_jaxpr/ppermute | solution.py:19
  243.3 15.5 %collective-permute-start.4 = (f32[192]{0:T(256)S(1)}, f32[192]{0:T(256)S(1)}, u32[]{:S(2)}, u32[]{:S(2)}) collective-permute-start(f32[192]{0:T(256)S(1)} %copy.58), channel_id=1, source_target_pairs={{0,16},{16,32},{32,48},{48,64},{64,80},{80,96},{96,112},{112,0},{1... | collective-permute-start | bytes 2312 | tf_op jit(solution)/shard_map/while/body/eval_jaxpr/ppermute | solution.py:19
  249.9 15.8 %collective-permute-start.5 = (f32[192,768]{1,0:T(8,128)S(1)}, f32[192,768]{1,0:T(8,128)S(1)}, u32[]{:S(2)}, u32[]{:S(2)}) collective-permute-start(f32[192,768]{1,0:T(8,128)S(1)} %convolution_add_fusion.2), channel_id=1, source_target_pairs={{0,16},{16,32},{32,48},{48,64},{64,80},{80,96},{96,112},{112,0},{1... | collective-permute-start | bytes 1769480 | tf_op jit(solution)/shard_map/while/body/eval_jaxpr/ppermute | solution.py:19
  265.7 15.7 %collective-permute-start.3 = (bf16[192,768]{1,0:T(8,128)(2,1)S(1)}, bf16[192,768]{1,0:T(8,128)(2,1)S(1)}, u32[]{:S(2)}, u32[]{:S(2)}) collective-permute-start(bf16[192,768]{1,0:T(8,128)(2,1)S(1)} %copy.57), channel_id=1, source_target_pairs={{0,16},{16,32},{32,48},{48,64},{64,80},{80,96},{96,112},{112,0},{1... | collective-permute-start | bytes 884744 | tf_op jit(solution)/shard_map/while/body/eval_jaxpr/ppermute | solution.py:19
  265.8 15.6 %collective-permute-start.4 = (f32[192]{0:T(256)S(1)}, f32[192]{0:T(256)S(1)}, u32[]{:S(2)}, u32[]{:S(2)}) collective-permute-start(f32[192]{0:T(256)S(1)} %copy.58), channel_id=1, source_target_pairs={{0,16},{16,32},{32,48},{48,64},{64,80},{80,96},{96,112},{112,0},{1... | collective-permute-start | bytes 2312 | tf_op jit(solution)/shard_map/while/body/eval_jaxpr/ppermute | solution.py:19
  272.5 15.1 %collective-permute-start.5 = (f32[192,768]{1,0:T(8,128)S(1)}, f32[192,768]{1,0:T(8,128)S(1)}, u32[]{:S(2)}, u32[]{:S(2)}) collective-permute-start(f32[192,768]{1,0:T(8,128)S(1)} %convolution_add_fusion.2), channel_id=1, source_target_pairs={{0,16},{16,32},{32,48},{48,64},{64,80},{80,96},{96,112},{112,0},{1... | collective-permute-start | bytes 1769480 | tf_op jit(solution)/shard_map/while/body/eval_jaxpr/ppermute | solution.py:19
  287.6 15.6 %collective-permute-start.3 = (bf16[192,768]{1,0:T(8,128)(2,1)S(1)}, bf16[192,768]{1,0:T(8,128)(2,1)S(1)}, u32[]{:S(2)}, u32[]{:S(2)}) collective-permute-start(bf16[192,768]{1,0:T(8,128)(2,1)S(1)} %copy.57), channel_id=1, source_target_pairs={{0,16},{16,32},{32,48},{48,64},{64,80},{80,96},{96,112},{112,0},{1... | collective-permute-start | bytes 884744 | tf_op jit(solution)/shard_map/while/body/eval_jaxpr/ppermute | solution.py:19
  287.7 15.5 %collective-permute-start.4 = (f32[192]{0:T(256)S(1)}, f32[192]{0:T(256)S(1)}, u32[]{:S(2)}, u32[]{:S(2)}) collective-permute-start(f32[192]{0:T(256)S(1)} %copy.58), channel_id=1, source_target_pairs={{0,16},{16,32},{32,48},{48,64},{64,80},{80,96},{96,112},{112,0},{1... | collective-permute-start | bytes 2312 | tf_op jit(solution)/shard_map/while/body/eval_jaxpr/ppermute | solution.py:19
  294.4 15.5 %collective-permute-start.5 = (f32[192,768]{1,0:T(8,128)S(1)}, f32[192,768]{1,0:T(8,128)S(1)}, u32[]{:S(2)}, u32[]{:S(2)}) collective-permute-start(f32[192,768]{1,0:T(8,128)S(1)} %convolution_add_fusion.2), channel_id=1, source_target_pairs={{0,16},{16,32},{32,48},{48,64},{64,80},{80,96},{96,112},{112,0},{1... | collective-permute-start | bytes 1769480 | tf_op jit(solution)/shard_map/while/body/eval_jaxpr/ppermute | solution.py:19
  309.8 15.6 %collective-permute-start.3 = (bf16[192,768]{1,0:T(8,128)(2,1)S(1)}, bf16[192,768]{1,0:T(8,128)(2,1)S(1)}, u32[]{:S(2)}, u32[]{:S(2)}) collective-permute-start(bf16[192,768]{1,0:T(8,128)(2,1)S(1)} %copy.57), channel_id=1, source_target_pairs={{0,16},{16,32},{32,48},{48,64},{64,80},{80,96},{96,112},{112,0},{1... | collective-permute-start | bytes 884744 | tf_op jit(solution)/shard_map/while/body/eval_jaxpr/ppermute | solution.py:19
  309.9 15.5 %collective-permute-start.4 = (f32[192]{0:T(256)S(1)}, f32[192]{0:T(256)S(1)}, u32[]{:S(2)}, u32[]{:S(2)}) collective-permute-start(f32[192]{0:T(256)S(1)} %copy.58), channel_id=1, source_target_pairs={{0,16},{16,32},{32,48},{48,64},{64,80},{80,96},{96,112},{112,0},{1... | collective-permute-start | bytes 2312 | tf_op jit(solution)/shard_map/while/body/eval_jaxpr/ppermute | solution.py:19
  316.6 16.3 %collective-permute-start.5 = (f32[192,768]{1,0:T(8,128)S(1)}, f32[192,768]{1,0:T(8,128)S(1)}, u32[]{:S(2)}, u32[]{:S(2)}) collective-permute-start(f32[192,768]{1,0:T(8,128)S(1)} %convolution_add_fusion.2), channel_id=1, source_target_pairs={{0,16},{16,32},{32,48},{48,64},{64,80},{80,96},{96,112},{112,0},{1... | collective-permute-start | bytes 1769480 | tf_op jit(solution)/shard_map/while/body/eval_jaxpr/ppermute | solution.py:19
  332.9 15.6 %collective-permute-start.3 = (bf16[192,768]{1,0:T(8,128)(2,1)S(1)}, bf16[192,768]{1,0:T(8,128)(2,1)S(1)}, u32[]{:S(2)}, u32[]{:S(2)}) collective-permute-start(bf16[192,768]{1,0:T(8,128)(2,1)S(1)} %copy.57), channel_id=1, source_target_pairs={{0,16},{16,32},{32,48},{48,64},{64,80},{80,96},{96,112},{112,0},{1... | collective-permute-start | bytes 884744 | tf_op jit(solution)/shard_map/while/body/eval_jaxpr/ppermute | solution.py:19
  333.0 15.5 %collective-permute-start.4 = (f32[192]{0:T(256)S(1)}, f32[192]{0:T(256)S(1)}, u32[]{:S(2)}, u32[]{:S(2)}) collective-permute-start(f32[192]{0:T(256)S(1)} %copy.58), channel_id=1, source_target_pairs={{0,16},{16,32},{32,48},{48,64},{64,80},{80,96},{96,112},{112,0},{1... | collective-permute-start | bytes 2312 | tf_op jit(solution)/shard_map/while/body/eval_jaxpr/ppermute | solution.py:19
  339.7 16.6 %collective-permute-start.5 = (f32[192,768]{1,0:T(8,128)S(1)}, f32[192,768]{1,0:T(8,128)S(1)}, u32[]{:S(2)}, u32[]{:S(2)}) collective-permute-start(f32[192,768]{1,0:T(8,128)S(1)} %convolution_add_fusion.2), channel_id=1, source_target_pairs={{0,16},{16,32},{32,48},{48,64},{64,80},{80,96},{96,112},{112,0},{1... | collective-permute-start | bytes 1769480 | tf_op jit(solution)/shard_map/while/body/eval_jaxpr/ppermute | solution.py:19
  356.4 15.6 %collective-permute-start.3 = (bf16[192,768]{1,0:T(8,128)(2,1)S(1)}, bf16[192,768]{1,0:T(8,128)(2,1)S(1)}, u32[]{:S(2)}, u32[]{:S(2)}) collective-permute-start(bf16[192,768]{1,0:T(8,128)(2,1)S(1)} %copy.57), channel_id=1, source_target_pairs={{0,16},{16,32},{32,48},{48,64},{64,80},{80,96},{96,112},{112,0},{1... | collective-permute-start | bytes 884744 | tf_op jit(solution)/shard_map/while/body/eval_jaxpr/ppermute | solution.py:19
  356.4 15.5 %collective-permute-start.4 = (f32[192]{0:T(256)S(1)}, f32[192]{0:T(256)S(1)}, u32[]{:S(2)}, u32[]{:S(2)}) collective-permute-start(f32[192]{0:T(256)S(1)} %copy.58), channel_id=1, source_target_pairs={{0,16},{16,32},{32,48},{48,64},{64,80},{80,96},{96,112},{112,0},{1... | collective-permute-start | bytes 2312 | tf_op jit(solution)/shard_map/while/body/eval_jaxpr/ppermute | solution.py:19
  363.1 16.3 %collective-permute-start.5 = (f32[192,768]{1,0:T(8,128)S(1)}, f32[192,768]{1,0:T(8,128)S(1)}, u32[]{:S(2)}, u32[]{:S(2)}) collective-permute-start(f32[192,768]{1,0:T(8,128)S(1)} %convolution_add_fusion.2), channel_id=1, source_target_pairs={{0,16},{16,32},{32,48},{48,64},{64,80},{80,96},{96,112},{112,0},{1... | collective-permute-start | bytes 1769480 | tf_op jit(solution)/shard_map/while/body/eval_jaxpr/ppermute | solution.py:19
  399.9 91.6 %copy-start = (bf16[192,768]{1,0:T(8,128)(2,1)S(1)}, bf16[192,768]{1,0:T(8,128)(2,1)}, u32[]{:S(2)}) copy-start(bf16[192,768]{1,0:T(8,128)(2,1)} %get-tuple-element.352) | copy-start | bytes 884740
  403.5 88.0 %collective-permute-start.8 = (f32[192,768]{1,0:T(8,128)S(1)}, f32[192,768]{1,0:T(8,128)S(1)}, u32[]{:S(2)}, u32[]{:S(2)}) collective-permute-start(f32[192,768]{1,0:T(8,128)S(1)} %add.142), channel_id=1, source_target_pairs={{0,16},{16,32},{32,48},{48,64},{64,80},{80,96},{96,112},{112,0},{1... | collective-permute-start | bytes 1769480 | tf_op jit(solution)/shard_map/ppermute | solution.py:19
  (62 other events, 287.2 us)
Sparse Core Ops, SparseCore 0:
  13.5 42.2 all-gather.3
  400.0 107.8 reduce-scatter.1
where the time goes:
time: 527 us; the launch traced here: 518 us
  matrix products  157 us (30%)
  waiting for transfers between devices  153 us (29%)
  blocking collectives  134 us (25%)
  other arithmetic  31.9 us (6%)
  between operations  16.8 us (3%)
  starting transfers between devices  11.7 us (2%)
  local copies, waits for them, and re-layouts  11.1 us (2%)
    ppermute x45, waiting for transfers between devices, shifted_2(): lax.ppermute(value, axis, [(i, (i + by) % peers) for i in range(peers)])  95.8 us
    psum x1, blocking collectives, per_device(): lax.psum(jnp.sum(row_lse + own_col - 2.0 * diagonal), ('outer', 'inner'))  87.3 us
    dot_general x16, matrix products, score_tile(): lax.dot_general(text_block, image_block, (((1,), (1,)), ((), ())), prefer...  83.1 us
    dot_general x8, matrix products, grad_terms(): jnp.dot(weights, image_block, preferred_element_type=jnp.float32)  62.9 us
    all_gather x2, blocking collectives, merged_2(): gathered = jax.tree.map(lambda a: lax.all_gather(a, axis), part)  47.1 us
    all_gather x1, waiting for transfers between devices, per_device(): text_group = lax.all_gather(text_rows, 'inner', axis=0, tiled=True)  41.6 us
    reduce_scatter x1, waiting for transfers between devices, per_device(): lax.psum_scatter(text_acc, 'inner', scatter_dimension=0, tiled=True)  15.6 us
    ppermute x45, starting transfers between devices, shifted_2(): lax.ppermute(value, axis, [(i, (i + by) % peers) for i in range(peers)])  11.6 us
  transfers between devices with their start and end apart: 47, of which 25 were waited for; matrix products, arithmetic and copies ran while one was open for 30% of the time, Pallas kernels for 0%

commit v1 on v0

v1 whole, which is shorter than its diff:
```python
import functools

import jax
import jax.numpy as jnp
from jax import lax
from jax.experimental import pallas as pl
from jax.experimental.pallas import tpu as pltpu
from jax.sharding import PartitionSpec as P

LOG2E = 1.4426950408889634
LN2 = 0.6931471805599453
UNIT = 2.0 ** -17
LOW = -1e30
Z_OFF = (0, 1, 3, 2)
GROUP = {off: g for g, off in enumerate(Z_OFF)}
SLOTS = ((0, 0), (0, 1), (0, 3), (1, 0), (0, 2), (1, 1), (1, 3), (1, 2))
SLOT = {pos: s for s, pos in enumerate(SLOTS)}
INNER = [(r, a, b) for r in range(4) for a in range(2) for b in range(2)]
MESSAGES = (
    ["tx", "ix", "xs", "xi"]
    + [f"tc{r}{a}" for r in range(4) for a in range(2)]
    + [f"{n}{d}{a}" for n in ("tz", "th", "iy", "ih", "zf", "yf") for d in "pm" for a in range(2)]
    + [f"{n}{d}" for n in ("zh", "yh") for d in "pm"]
    + [f"cs{g}" for g in range(4)]
    + [f"{n}{s}" for n in ("lr", "lo") for s in range(1, 8)]
    + [f"{n}{q}" for n in ("lc", "li") for q in range(1, 16)]
)
SEM = {name: i for i, name in enumerate(MESSAGES)}


def dot_nt(a, b):
    return lax.dot_general(a, b, (((1,), (1,)), ((), ())), preferred_element_type=jnp.float32)


def dot_nn(a, b):
    return jnp.dot(a, b, preferred_element_type=jnp.float32)


def dot_tn(a, b):
    return lax.dot_general(a, b, (((0,), (0,)), ((), ())), preferred_element_type=jnp.float32)


def kernel(
    ic_ref, ie_ref, tc_ref, te_ref, scale_ref, loss_ref, ig_ref, tg_ref,
    T, I, S, W, mr, sr, mc, sc, lrep, lcol, LR, LC, LO, LI,
    CS, CR, ZS, ZH, ZF, YS, YH, YF, XS, XR, dsum, send_sems, recv_sems,
):
    R, D = ic_ref.shape
    H = R // 2
    G = 4 * R
    RP = LR.shape[2]
    NT = G // 128
    ND = D // 128

    outer = lax.axis_index("outer")
    inner = lax.axis_index("inner")
    xh, y = outer // 4, outer % 4
    z, xl, c = inner // 4, (inner // 2) % 2, inner % 2

    def at(dh=0, dy=0, dz=0, dl=0, dc=0):
        h = xh if dh == 0 else 1 - xh
        l = xl if dl == 0 else 1 - xl
        k = c if dc == 0 else 1 - c
        return (h * 4 + (y + dy) % 4, ((z + dz) % 4) * 4 + l * 2 + k)

    outer_peers = [(s, SLOTS[s]) for s in range(1, 8)]
    inner_peers = [(q, INNER[q]) for q in range(1, 16)]
    barrier = pltpu.get_barrier_semaphore()
    for _, (a, r) in outer_peers:
        pl.semaphore_signal(barrier, inc=1, device_id=at(dh=a, dy=r), device_id_type=pl.DeviceIdType.MESH)
    for _, (r, a, b) in inner_peers:
        pl.semaphore_signal(
            barrier, inc=1, device_id=at(dz=r, dl=a, dc=b), device_id_type=pl.DeviceIdType.MESH
        )

    def copy(name, src, dst, device):
        return pltpu.make_async_remote_copy(
            src_ref=src, dst_ref=dst, send_sem=send_sems.at[SEM[name]], recv_sem=recv_sems.at[SEM[name]],
            device_id=device, device_id_type=pl.DeviceIdType.MESH,
        )

    started = {}

    def send(name, src, dst, device):
        started[name] = copy(name, src, dst, device)
        started[name].start()

    def got(name):
        started[name].wait_recv()

    def trow(a, b):
        l = xl if a == 0 else 1 - xl
        k = c if b == 0 else 1 - c
        return pl.multiple_of((l * 2 + k) * R, R)

    def tblock(r, a, b=0):
        return T.at[GROUP[r], pl.ds(trow(a, b), R), :]

    def thalf(r, a, half):
        return T.at[GROUP[r], pl.ds(pl.multiple_of(trow(a, 0) + half * H, H), H), :]

    def iblock(a, r):
        return I.at[pl.ds(SLOT[a, r] * R, R), :]

    def ihalf(a, r, half):
        return I.at[pl.ds(SLOT[a, r] * R + half * H, H), :]

    def decode(codes_ref, exps_ref, f):
        codes = codes_ref[:, f * 128 : (f + 1) * 128]
        field = (codes >> 3) & 15
        mantissa = codes & 7
        significand = jnp.where(field > 0, mantissa + 8, mantissa)
        shift = jnp.maximum(field, 1) - 1 + (exps_ref[:, f : f + 1] + 8)
        magnitude = (significand << shift).astype(jnp.float32) * UNIT
        return jnp.where(codes > 127, -magnitude, magnitude)

    own_rows = trow(0, 0)
    diag = jnp.zeros((R, 128), jnp.float32)
    for f in range(ND):
        image = decode(ic_ref, ie_ref, f)
        text = decode(tc_ref, te_ref, f)
        diag = diag + image * text
        I[0:R, f * 128 : (f + 1) * 128] = image.astype(jnp.bfloat16)
        T[0, pl.ds(own_rows, R), f * 128 : (f + 1) * 128] = text.astype(jnp.bfloat16)
    dsum[0:R, :] = diag
    if RP > R:
        dsum[R:RP, :] = jnp.zeros((RP - R, 128), jnp.float32)
        for s in range(8):
            mr[s, R:RP, :] = jnp.zeros((RP - R, 128), jnp.float32)
            sr[s, R:RP, :] = jnp.ones((RP - R, 128), jnp.float32)
    for s in range(8):
        mr[s, 0:R, :] = jnp.full((R, 128), LOW, jnp.float32)
        sr[s, 0:R, :] = jnp.zeros((R, 128), jnp.float32)
    mc[...] = jnp.full(mc.shape, LOW, jnp.float32)
    sc[...] = jnp.zeros(sc.shape, jnp.float32)
    k = scale_ref[0]
    k2 = k * LOG2E

    pl.semaphore_wait(barrier, 22)

    def s_unit(g, slot):
        rows = pl.ds(pl.multiple_of(slot * R, R), R)
        tile = dot_nt(I[rows, :], T[g]) * k2
        S[g, rows, :] = tile
        parts = [tile[:, j * 128 : (j + 1) * 128] for j in range(NT)]
        old = mr[slot, 0:R, :]
        top = functools.reduce(jnp.maximum, parts, old)
        total = sr[slot, 0:R, :] * jnp.exp2(old - top)
        for part in parts:
            total = total + jnp.exp2(part - top)
        mr[slot, 0:R, :] = top
        sr[slot, 0:R, :] = total
        cols = tile.reshape(R // 8, 8, G)
        old = mc[g]
        top = jnp.maximum(old, jnp.max(cols, axis=0))
        sc[g] = sc[g] * jnp.exp2(old - top) + jnp.sum(jnp.exp2(cols - top[None]), axis=0)
        mc[g] = top

    def s_units(g, lo, hi):
        lax.fori_loop(lo, hi, lambda slot, _: (s_unit(g, slot), 0)[1], 0)

    send("tzm0", tblock(0, 0), tblock(3, 0), at(dz=1))
    send("tzp0", tblock(0, 0), tblock(1, 0), at(dz=3))
    send("iym0", iblock(0, 0), iblock(0, 3), at(dy=1))
    send("iyp0", iblock(0, 0), iblock(0, 1), at(dy=3))
    send("tx", tblock(0, 0), tblock(0, 0), at(dl=1))
    send("ix", iblock(0, 0), iblock(1, 0), at(dh=1))
    send("tc00", tblock(0, 0), tblock(0, 0), at(dc=1))

    def to_core(r, a):
        send(f"tc{r}{a}", tblock(r, a), tblock(r, a), at(dc=1))

    def forward(a):
        got(f"tzm{a}")
        send(f"thm{a}", thalf(3, a, 0), thalf(2, a, 0), at(dz=1))
        got(f"tzp{a}")
        send(f"thp{a}", thalf(1, a, 1), thalf(2, a, 1), at(dz=3))
        to_core(3, a)
        to_core(1, a)
        got(f"iym{a}")
        send(f"ihm{a}", ihalf(a, 3, 0), ihalf(a, 2, 0), at(dy=1))
        got(f"iyp{a}")
        send(f"ihp{a}", ihalf(a, 1, 1), ihalf(a, 2, 1), at(dy=3))

    def arrived(a):
        got(f"thm{a}")
        got(f"thp{a}")
        to_core(2, a)
        got(f"ihm{a}")
        got(f"ihp{a}")

    forward(0)
    got("tx")
    send("tzm1", tblock(0, 1), tblock(3, 1), at(dz=1))
    send("tzp1", tblock(0, 1), tblock(1, 1), at(dz=3))
    to_core(0, 1)
    got("ix")
    send("iym1", iblock(1, 0), iblock(1, 3), at(dy=1))
    send("iyp1", iblock(1, 0), iblock(1, 1), at(dy=3))
    got("tc00")
    got("tc01")
    s_units(0, 0, 4)
    arrived(0)
    s_units(0, 4, 5)
    forward(1)
    for name in ("tc10", "tc11", "tc30", "tc31"):
        got(name)
    s_units(0, 5, 7)
    s_units(1, 0, 7)
    s_units(2, 0, 7)
    arrived(1)
    s_units(0, 7, 8)
    s_units(1, 7, 8)
    s_units(2, 7, 8)
    got("tc20")
    got("tc21")
    s_units(3, 0, 8)

    for s in range(8):
        m = mr[s].T
        top = jnp.max(m, axis=0, keepdims=True)
        total = jnp.sum(sr[s].T * jnp.exp2(m - top), axis=0, keepdims=True)
        LR[0, s : s + 1, :] = top + jnp.log(total) * LOG2E
    for s, (a, r) in outer_peers:
        send(f"lr{s}", LR.at[0], LR.at[SLOT[a, -r % 4]], at(dh=a, dy=r))
    for g in range(4):
        m = mc[g]
        top = jnp.max(m, axis=0, keepdims=True)
        total = jnp.sum(sc[g] * jnp.exp2(m - top), axis=0, keepdims=True)
        LC[0, g : g + 1, :] = top + jnp.log(total) * LOG2E
    for q, (r, a, b) in inner_peers:
        send(f"lc{q}", LC.at[0], LC.at[INNER.index((-r % 4, a, b))], at(dz=r, dl=a, dc=b))

    def merge(parts):
        top = functools.reduce(jnp.maximum, parts)
        total = functools.reduce(jnp.add, [jnp.exp2(part - top) for part in parts])
        return top + jnp.log(total) * LOG2E

    for s, _ in outer_peers:
        got(f"lr{s}")
    row_own = None
    for s, (a, r) in enumerate(SLOTS):
        parts = []
        for p, (da, dr) in enumerate(SLOTS):
            there = SLOT[a ^ da, (r - dr) % 4]
            parts.append(LR[p, there : there + 1, :])
        lse = merge(parts)
        if s == 0:
            row_own = lse
        lrep[s] = jnp.broadcast_to(lse + 1.0, (128, RP)).T
    for q, _ in inner_peers:
        got(f"lc{q}")
    col_own = None
    for g, r in enumerate(Z_OFF):
        parts = []
        for q, (dr, _, _) in enumerate(INNER):
            there = GROUP[(r - dr) % 4]
            parts.append(LC[q, there : there + 1, :])
        lse = merge(parts)
        if g == 0:
            col_own = lse
        lcol[g] = jnp.broadcast_to(lse + 1.0, (8, G))

    block = xl * 2 + c
    col_mine = col_own[:, 0:R]
    for b in range(1, 4):
        col_mine = jnp.where(block == b, col_own[:, b * R : (b + 1) * R], col_mine)
    diag_own = jnp.sum(dsum[...].T, axis=0, keepdims=True)[:, 0:R] * k2
    loss_here = jnp.sum(row_own[:, 0:R] + col_mine - 2.0 * diag_own)
    LO[0] = jnp.full((8, 128), loss_here, jnp.float32)
    for s, (a, r) in outer_peers:
        send(f"lo{s}", LO.at[0], LO.at[SLOT[a, -r % 4]], at(dh=a, dy=r))

    def w_unit(g, slot):
        rows = pl.ds(pl.multiple_of(slot * R, R), R)
        by_row = lrep[slot, 0:R, :]
        for j in range(NT):
            cols = slice(j * 128, (j + 1) * 128)
            s = S[g, rows, cols]
            w = jnp.exp2(s - by_row) + jnp.exp2(s - lcol[g, 0:1, cols])
            W[g, rows, cols] = w.astype(jnp.bfloat16)

    def w_units(g, lo, hi):
        lax.fori_loop(lo, hi, lambda slot, _: (w_unit(g, slot), 0)[1], 0)

    TW = 384 if G % 384 == 0 else 128

    def t_terms(g):
        def step(j, _):
            cols = pl.ds(pl.multiple_of(j * TW, TW), TW)
            S[g, cols, :] = dot_tn(W[g, :, cols], I[...])
            return 0

        lax.fori_loop(0, G // TW, step, 0)
        for a in range(2):
            CS[g, a] = S[g, pl.ds(trow(a, 1), R), :].astype(jnp.bfloat16)
        send(f"cs{g}", CS.at[g], CR.at[g], at(dc=1))

    def t_sum(g, a):
        return S[g, pl.ds(trow(a, 0), R), :] + CR[g, a].astype(jnp.float32)

    def i_terms(slot):
        rows = slice(slot * R, (slot + 1) * R)
        total = dot_nn(W[0, rows, :], T[0])
        for g in range(1, 4):
            total = total + dot_nn(W[g, rows, :], T[g])
        return total

    w_units(3, 0, 8)
    t_terms(3)
    for g in range(3):
        w_units(g, 4, 5)
        w_units(g, 7, 8)
    for a in range(2):
        term = i_terms(SLOT[a, 2]).astype(jnp.bfloat16)
        YS[0, 0, a] = term[0:H]
        YS[0, 1, a] = term[H:R]
    send("yhm", YS.at[0, 0], YH.at[0], at(dy=1))
    send("yhp", YS.at[0, 1], YH.at[1], at(dy=3))
    got("cs3")
    for a in range(2):
        term = t_sum(3, a).astype(jnp.bfloat16)
        ZS[0, 0, a] = term[0:H]
        ZS[0, 1, a] = term[H:R]
    send("zhm", ZS.at[0, 0], ZH.at[0], at(dz=1))
    send("zhp", ZS.at[0, 1], ZH.at[1], at(dz=3))

    w_units(1, 0, 4)
    w_units(1, 5, 7)
    t_terms(1)
    w_units(2, 0, 4)
    w_units(2, 5, 7)
    t_terms(2)

    def near(index, half, a, term, held, out):
        for h in range(2):
            part = term[h * H : (h + 1) * H]
            if h == half:
                part = part + held[half, a].astype(jnp.float32)
            out[index, h, a] = part.astype(jnp.bfloat16)

    got("cs1")
    got("zhm")
    for a in (1, 0):
        near(1, 0, a, t_sum(1, a), ZH, ZS)
        send(f"zfm{a}", ZS.at[1, :, a], ZF.at[0, a], at(dz=1))
    got("cs2")
    got("zhp")
    for a in (1, 0):
        near(2, 1, a, t_sum(2, a), ZH, ZS)
        send(f"zfp{a}", ZS.at[2, :, a], ZF.at[1, a], at(dz=3))
    w_units(0, 0, 4)
    w_units(0, 5, 7)
    got("yhm")
    for a in (1, 0):
        near(1, 0, a, i_terms(SLOT[a, 1]), YH, YS)
        send(f"yfm{a}", YS.at[1, :, a], YF.at[0, a], at(dy=1))
    got("yhp")
    for a in (1, 0):
        near(2, 1, a, i_terms(SLOT[a, 3]), YH, YS)
        send(f"yfp{a}", YS.at[2, :, a], YF.at[1, a], at(dy=3))
    t_terms(0)

    for s, _ in outer_peers:
        got(f"lo{s}")

    def ring(values):
        return (values[0] + values[2]) + (values[1] + values[3])

    outer_loss = ring([LO[SLOT[0, r]] for r in range(4)]) + ring([LO[SLOT[1, r]] for r in range(4)])
    LI[0] = outer_loss
    for q, (r, a, b) in inner_peers:
        send(f"li{q}", LI.at[0], LI.at[INNER.index((-r % 4, a, b))], at(dz=r, dl=a, dc=b))

    ig_ref[...] = i_terms(SLOT[0, 0])
    far = i_terms(SLOT[1, 0])

    def both(held, a, term):
        halves = []
        for h in range(2):
            part = term[h * H : (h + 1) * H]
            halves.append(part + (held[0, a, h].astype(jnp.float32) + held[1, a, h].astype(jnp.float32)))
        return halves

    got("cs0")
    got("zfm1")
    got("zfp1")
    for h, part in enumerate(both(ZF, 1, t_sum(0, 1))):
        XS[0, h * H : (h + 1) * H, :] = part.astype(jnp.bfloat16)
    send("xs", XS.at[0], XR.at[0], at(dl=1))
    got("yfm1")
    got("yfp1")
    for h, part in enumerate(both(YF, 1, far)):
        XS[1, h * H : (h + 1) * H, :] = part.astype(jnp.bfloat16)
    send("xi", XS.at[1], XR.at[1], at(dh=1))

    for q, _ in inner_peers:
        got(f"li{q}")
    by_z = []
    for r in range(4):
        v = [[LI[INNER.index((r, a, b))] for b in range(2)] for a in range(2)]
        by_z.append((v[0][0] + v[0][1]) + (v[1][0] + v[1][1]))
    loss_ref[...] = ring(by_z) * (LN2 / (2 * 128 * R))

    got("zfm0")
    got("zfp0")
    text_parts = both(ZF, 0, t_sum(0, 0))
    got("xs")
    for h, part in enumerate(text_parts):
        rows = slice(h * H, (h + 1) * H)
        total = part + XR[0, rows, :].astype(jnp.float32)
        tg_ref[rows, :] = k * (total - I[rows, :].astype(jnp.float32))
    got("yfm0")
    got("yfp0")
    image_parts = both(YF, 0, ig_ref[...])
    got("xi")
    for h, part in enumerate(image_parts):
        rows = slice(h * H, (h + 1) * H)
        total = part + XR[1, rows, :].astype(jnp.float32)
        text = T[0, pl.ds(pl.multiple_of(own_rows + h * H, H), H), :]
        ig_ref[rows, :] = k * (total - text.astype(jnp.float32))
    for name in started:
        started[name].wait_send()


def per_device(image_codes, image_exps, text_codes, text_exps, logit_scale):
    R, D = image_codes.shape
    H = R // 2
    G = 4 * R
    RP = -(-R // 128) * 128
    bf16, f32 = jnp.bfloat16, jnp.float32
    vmem = pl.BlockSpec(memory_space=pltpu.VMEM)
    scratch = [
        pltpu.VMEM((4, G, D), bf16),
        pltpu.VMEM((8 * R, D), bf16),
        pltpu.VMEM((4, 8 * R, G), f32),
        pltpu.VMEM((4, 8 * R, G), bf16),
        pltpu.VMEM((8, RP, 128), f32),
        pltpu.VMEM((8, RP, 128), f32),
        pltpu.VMEM((4, 8, G), f32),
        pltpu.VMEM((4, 8, G), f32),
        pltpu.VMEM((8, RP, 128), f32),
        pltpu.VMEM((4, 8, G), f32),
        pltpu.VMEM((8, 8, RP), f32),
        pltpu.VMEM((16, 4, G), f32),
        pltpu.VMEM((8, 8, 128), f32),
        pltpu.VMEM((16, 8, 128), f32),
        pltpu.VMEM((4, 2, R, D), bf16),
        pltpu.VMEM((4, 2, R, D), bf16),
        pltpu.VMEM((3, 2, 2, H, D), bf16),
        pltpu.VMEM((2, 2, H, D), bf16),
        pltpu.VMEM((2, 2, 2, H, D), bf16),
        pltpu.VMEM((3, 2, 2, H, D), bf16),
        pltpu.VMEM((2, 2, H, D), bf16),
        pltpu.VMEM((2, 2, 2, H, D), bf16),
        pltpu.VMEM((2, R, D), bf16),
        pltpu.VMEM((2, R, D), bf16),
        pltpu.VMEM((RP, 128), f32),
        pltpu.SemaphoreType.DMA((len(MESSAGES),)),
        pltpu.SemaphoreType.DMA((len(MESSAGES),)),
    ]
    loss, image_grad, text_grad = pl.pallas_call(
        kernel,
        out_shape=[
            jax.ShapeDtypeStruct((8, 128), f32),
            jax.ShapeDtypeStruct((R, D), f32),
            jax.ShapeDtypeStruct((R, D), f32),
        ],
        in_specs=[vmem, vmem, vmem, vmem, pl.BlockSpec(memory_space=pltpu.SMEM)],
        out_specs=[vmem, vmem, vmem],
        scratch_shapes=scratch,
        compiler_params=pltpu.CompilerParams(
            collective_id=0, has_side_effects=True, vmem_limit_bytes=63 * 1024 * 1024
        ),
    )(image_codes, image_exps, text_codes, text_exps, logit_scale)
    return loss[0, 0], image_grad, text_grad


def solution(mesh):
    rows = P(("outer", "inner"), None)
    return jax.shard_map(
        per_device, mesh=mesh, in_specs=(rows, rows, rows, rows, P()), out_specs=(P(), rows, rows), check_vma=False
    )
```

time: 527 us -> 111 us (0.21); the launches traced: 518 us -> 111 us
  matrix products: 157 us -> 0 us
  waiting for transfers between devices: 153 us -> 0 us
  blocking collectives: 134 us -> 0 us
  Pallas kernels: 0 us -> 104 us
  other arithmetic: 31.9 us -> 0 us
  between operations: 16.8 us -> 1.3 us
  starting transfers between devices: 11.7 us -> 0 us
    dot_general x32 -> x0, matrix products: 157 us -> none  [the longest x16 83.1 us: score_tile(): lax.dot_general(text_block, image_block, (((1,), (1,)), ((), ())), prefer...]
    pallas_call x0 -> x1, Pallas kernels: none -> 104 us  [per_device(): pl.pallas_call(kernel, out_shape=[jax.ShapeDtypeStruct((8, 128), f32), ja...]
    ppermute x45 -> x0, waiting for transfers between devices: 95.8 us -> none  [shifted_2(): lax.ppermute(value, axis, [(i, (i + by) % peers) for i in range(peers)])]
    psum x1 -> x0, blocking collectives: 87.3 us -> none  [per_device(): lax.psum(jnp.sum(row_lse + own_col - 2.0 * diagonal), ('outer', 'inner'))]
    all_gather x2 -> x0, blocking collectives: 47.1 us -> none  [merged_2(): gathered = jax.tree.map(lambda a: lax.all_gather(a, axis), part)]
    all_gather x1 -> x0, waiting for transfers between devices: 41.6 us -> none  [per_device(): text_group = lax.all_gather(text_rows, 'inner', axis=0, tiled=True)]
    reduce_scatter x1 -> x0, waiting for transfers between devices: 15.6 us -> none  [per_device(): lax.psum_scatter(text_acc, 'inner', scatter_dimension=0, tiled=True)]
    add x34 -> x0, other arithmetic: 11.7 us -> none  [the longest x1 11.2 us: second_visit(): text_acc + text_term]
  transfers between devices with their start and end apart: 47 -> 0, of which waited for: 25 -> 0; matrix products, arithmetic and copies ran while one was open for 30% -> 0% of each run, Pallas kernels for 0% -> 0%
where the time goes in v1:
time: 111 us
  Pallas kernels  104 us (94%)
  local copies, waits for them, and re-layouts  6.23 us (6%)
  between operations  1.3 us (1%)
    pallas_call x1, Pallas kernels, per_device(): pl.pallas_call(kernel, out_shape=[jax.ShapeDtypeStruct((8, 128), f32), ja...  104 us
    unnamed x8, local copies, waits for them, and re-layouts  5.03 us

profile of v1, /device:TPU:1, one launch (start us, length us, event | category | flops | bytes accessed | tf_op | source)
XLA Modules:
  0.0 111.3 jit_solution(11074785584758518860)
XLA Ops:
  1.3 0.0 copy-start.1
  1.3 1.5 %copy.8.ie_ref = s32[192,6]{1,0:T(8,128)} copy(s32[192,6]{0,1:T(8,128)} %param.6) | data formatting | bytes 9216 | tf_op args[1]
  2.8 0.0 copy-done.1
  2.8 0.8 copy.9.te_ref
  3.5 103.7 %shard_map.76 = (f32[8,128]{1,0:T(8,128)}, f32[192,768]{1,0:T(8,128)}, f32[192,768]{1,0:T(8,128)}) custom-call(s32[192,768]{1,0:T(8,128)} %ic_ref.1, s32[192,6]{1,0:T(8,128)} %copy.8.ie_ref, s32[192,768]{1,0:T(8,128)} %tc_ref.1, s32[192,6]{1,0:T(8,128)} %copy.9.te_ref, f32[1]{0:T(128)S(6)} %copy.12.scale_ref), custom_call_target="tpu_custom_call" | custom-call | tf_op jit(solution)/shard_map/pallas_call | solution.py:462
  107.3 1.2 %slice.3 = f32[1,1]{1,0:T(1,128)} slice(f32[8,128]{1,0:T(8,128)} %get-tuple-element.6), slice={[0:1], [0:1]} | slice | bytes 8 | tf_op jit(solution)/shard_map/slice | solution.py:476
  108.5 0.0 copy-start
  108.5 2.0 %copy.13 = f32[192,768]{1,0:T(8,128)} copy(f32[192,768]{1,0:T(8,128)} %get-tuple-element.13) | data formatting | bytes 1179648
  110.4 0.0 copy-done
  110.4 0.8 copy.14
Async XLA Ops:
  1.3 1.5 %copy-start.1 = (s32[192,6]{0,1:T(8,128)S(1)}, s32[192,6]{0,1:T(8,128)}, u32[]{:S(2)}) copy-start(s32[192,6]{0,1:T(8,128)} %param.8) | copy-start | bytes 13828
  108.5 2.0 %copy-start = (f32[192,768]{1,0:T(8,128)S(1)}, f32[192,768]{1,0:T(8,128)}, u32[]{:S(2)}) copy-start(f32[192,768]{1,0:T(8,128)} %get-tuple-element.14) | copy-start | bytes 1769476

commit v2 on v1

v2 whole, which is shorter than its diff:
```python
import functools

import jax
import jax.numpy as jnp
from jax import lax
from jax.experimental import pallas as pl
from jax.experimental.pallas import tpu as pltpu
from jax.sharding import PartitionSpec as P

LOG2E = 1.4426950408889634
LN2 = 0.6931471805599453
UNIT = 2.0 ** -17
LOW = -1e30
Z_OFF = (0, 1, 3, 2)
GROUP = {off: g for g, off in enumerate(Z_OFF)}
SLOTS = ((0, 0), (0, 1), (0, 3), (0, 2), (1, 0), (1, 1), (1, 3), (1, 2))
SLOT = {pos: s for s, pos in enumerate(SLOTS)}
INNER = [(r, a, b) for r in range(4) for a in range(2) for b in range(2)]
MESH = pl.DeviceIdType.MESH
MESSAGES = (
    [f"{n}{h}" for n in ("tx", "ix", "xs", "xi") for h in range(2)]
    + [f"tc{r}{a}" for r in range(4) for a in range(2)]
    + [f"{n}{d}{a}{h}" for n in ("tz", "iy", "zn", "yn") for d in "pm" for a in range(2) for h in range(2)]
    + [f"{n}{d}{a}" for n in ("th", "ih", "zh", "yh") for d in "pm" for a in range(2)]
    + [f"cs{a}{g}" for a in range(2) for g in range(4)]
    + [f"{n}{s}" for n in ("lr", "lo") for s in range(1, 8)]
    + [f"{n}{q}" for n in ("lc", "li") for q in range(1, 16)]
)
SEM = {name: i for i, name in enumerate(MESSAGES)}


def dot_nt(a, b):
    return lax.dot_general(a, b, (((1,), (1,)), ((), ())), preferred_element_type=jnp.float32)


def dot_nn(a, b):
    return jnp.dot(a, b, preferred_element_type=jnp.float32)


def dot_tn(a, b):
    return lax.dot_general(a, b, (((0,), (0,)), ((), ())), preferred_element_type=jnp.float32)


def kernel(
    ic_ref, ie_ref, tc_ref, te_ref, scale_ref, loss_ref, ig_ref, tg_ref,
    T, I, S, W, mr, sr, mc, sc, lcol, LR, LC, LO, LI,
    PT, CR, ZS, ZH, ZN, YS, YH, YN, XS, XR, dsum, exps, send_sems, recv_sems,
):
    R, D = ic_ref.shape
    H = R // 2
    Q = 2 * R
    C = 8 * R
    RP = LR.shape[2]
    ND = D // 128
    NB = ie_ref.shape[0]

    outer = lax.axis_index("outer")
    inner = lax.axis_index("inner")
    xh, y = outer // 4, outer % 4
    z, xl, c = inner // 4, (inner // 2) % 2, inner % 2

    def at(dh=0, dy=0, dz=0, dl=0, dc=0):
        h = xh if dh == 0 else 1 - xh
        l = xl if dl == 0 else 1 - xl
        k = c if dc == 0 else 1 - c
        return (h * 4 + (y + dy) % 4, ((z + dz) % 4) * 4 + l * 2 + k)

    outer_peers = [(s, SLOTS[s]) for s in range(1, 8)]
    inner_peers = [(q, INNER[q]) for q in range(1, 16)]
    barrier = pltpu.get_barrier_semaphore()
    for _, (a, r) in outer_peers:
        pl.semaphore_signal(barrier, inc=1, device_id=at(dh=a, dy=r), device_id_type=MESH)
    for _, (r, a, b) in inner_peers:
        pl.semaphore_signal(barrier, inc=1, device_id=at(dz=r, dl=a, dc=b), device_id_type=MESH)

    started = {}

    def send(name, src, dst, device):
        started[name] = pltpu.make_async_remote_copy(
            src_ref=src, dst_ref=dst, send_sem=send_sems.at[SEM[name]], recv_sem=recv_sems.at[SEM[name]],
            device_id=device, device_id_type=MESH,
        )
        started[name].start()

    def got(*names):
        for name in names:
            started[name].wait_recv()

    def core_row(b):
        return pl.multiple_of((c if b == 0 else 1 - c) * R, R)

    def trows(r, b, h=None):
        first = GROUP[r] * Q + core_row(b)
        if h is None:
            return pl.ds(pl.multiple_of(first, R), R)
        return pl.ds(pl.multiple_of(first + h * H, H), H)

    def tpart(a, r, h=None):
        return T.at[a, trows(r, 0, h), :]

    def ipart(a, r, h):
        return I.at[pl.ds(SLOT[a, r] * R + h * H, H), :]

    def columns(exps_ref):
        exps[0:NB, 0:R] = exps_ref[...]
        return exps[...].T

    def decode(codes_ref, exps_by_row, f):
        codes = codes_ref[:, f * 128 : (f + 1) * 128]
        field = (codes >> 3) & 15
        mantissa = codes & 7
        significand = jnp.where(field > 0, mantissa + 8, mantissa)
        shift = jnp.maximum(field, 1) - 1 + (exps_by_row[0:R, f : f + 1] + 8)
        magnitude = (significand << shift).astype(jnp.float32) * UNIT
        return jnp.where(codes > 127, -magnitude, magnitude)

    exps[...] = jnp.zeros(exps.shape, jnp.int32)
    image_exps = columns(ie_ref)
    text_exps = columns(te_ref)
    diag = jnp.zeros((R, 128), jnp.float32)
    for f in range(ND):
        image = decode(ic_ref, image_exps, f)
        text = decode(tc_ref, text_exps, f)
        diag = diag + image * text
        I[0:R, f * 128 : (f + 1) * 128] = image.astype(jnp.bfloat16)
        T[0, trows(0, 0), f * 128 : (f + 1) * 128] = text.astype(jnp.bfloat16)

    pl.semaphore_wait(barrier, 22)

    def ring_t(a, d, h):
        far = 1 if d == "m" else 3
        send(f"tz{d}{a}{h}", tpart(a, 0, h), tpart(a, -far % 4, h), at(dz=far))

    def ring_i(a, d, h):
        far = 1 if d == "m" else 3
        send(f"iy{d}{a}{h}", ipart(a, 0, h), ipart(a, -far % 4, h), at(dy=far))

    def on_t(a, d):
        far, h = (1, 0) if d == "m" else (3, 1)
        got(f"tz{d}{a}{h}")
        send(f"th{d}{a}", tpart(a, -far % 4, h), tpart(a, 2, h), at(dz=far))

    def on_i(a, d):
        far, h = (1, 0) if d == "m" else (3, 1)
        got(f"iy{d}{a}{h}")
        send(f"ih{d}{a}", ipart(a, -far % 4, h), ipart(a, 2, h), at(dy=far))

    def to_core(r, a):
        send(f"tc{r}{a}", tpart(a, r), tpart(a, r), at(dc=1))

    for d in "mp":
        ring_t(0, d, 0 if d == "m" else 1)
        ring_i(0, d, 0 if d == "m" else 1)
    for h in range(2):
        send(f"tx{h}", tpart(0, 0, h), tpart(1, 0, h), at(dl=1))
    for d in "mp":
        ring_t(0, d, 1 if d == "m" else 0)
        ring_i(0, d, 1 if d == "m" else 0)
    for h in range(2):
        send(f"ix{h}", ipart(0, 0, h), ipart(1, 0, h), at(dh=1))
    to_core(0, 0)

    dsum[0:R, :] = diag
    if RP > R:
        dsum[R:RP, :] = jnp.zeros((RP - R, 128), jnp.float32)
        for s in range(8):
            mr[s, R:RP, :] = jnp.zeros((RP - R, 128), jnp.float32)
            sr[s, R:RP, :] = jnp.ones((RP - R, 128), jnp.float32)
    for s in range(8):
        mr[s, 0:R, :] = jnp.full((R, 128), LOW, jnp.float32)
        sr[s, 0:R, :] = jnp.zeros((R, 128), jnp.float32)
    mc[...] = jnp.full(mc.shape, LOW, jnp.float32)
    sc[...] = jnp.zeros(sc.shape, jnp.float32)
    k = scale_ref[0]
    k2 = k * LOG2E

    def s_tile(a, lo, hi, first, last):
        rows, cols = slice(lo * R, hi * R), slice(first * Q, last * Q)
        tile = dot_nt(I[rows, :], T[a, cols, :]) * k2
        S[a, rows, cols] = tile
        parts = [tile[:, j : j + 128].reshape(hi - lo, R, 128) for j in range(0, (last - first) * Q, 128)]
        old = mr[lo:hi, 0:R, :]
        top = functools.reduce(jnp.maximum, parts, old)
        total = sr[lo:hi, 0:R, :] * jnp.exp2(old - top)
        for part in parts:
            total = total + jnp.exp2(part - top)
        mr[lo:hi, 0:R, :] = top
        sr[lo:hi, 0:R, :] = total
        by_col = tile.reshape((hi - lo) * R // 8, 8, (last - first) * Q)
        old = mc[a, :, cols]
        top = jnp.maximum(old, jnp.max(by_col, axis=0))
        sc[a, :, cols] = sc[a, :, cols] * jnp.exp2(old - top) + jnp.sum(jnp.exp2(by_col - top[None]), axis=0)
        mc[a, :, cols] = top

    on_t(0, "m")
    on_t(0, "p")
    on_i(0, "m")
    on_i(0, "p")
    got("tx0")
    ring_t(1, "m", 0)
    got("tx1")
    ring_t(1, "p", 1)
    ring_t(1, "m", 1)
    ring_t(1, "p", 0)
    to_core(0, 1)
    got("tzm01")
    to_core(3, 0)
    got("tzp00")
    to_core(1, 0)
    got("iym01", "iyp00", "tc00", "tc30", "tc10")
    s_tile(0, 0, 3, 0, 2)
    s_tile(0, 0, 3, 2, 3)
    got("thm0", "thp0")
    to_core(2, 0)
    got("ihm0", "ihp0", "ix0")
    ring_i(1, "m", 0)
    ring_i(1, "p", 0)
    s_tile(0, 3, 4, 0, 3)
    got("tc01")
    s_tile(1, 0, 4, 0, 1)
    got("ix1")
    ring_i(1, "m", 1)
    ring_i(1, "p", 1)
    on_t(1, "m")
    on_t(1, "p")
    got("tc20")
    s_tile(0, 0, 4, 3, 4)
    s_tile(0, 4, 5, 0, 4)
    got("tzm11")
    to_core(3, 1)
    got("tzp10")
    to_core(1, 1)
    on_i(1, "m")
    s_tile(1, 4, 5, 0, 1)
    got("tc31", "tc11")
    s_tile(1, 0, 5, 1, 3)
    on_i(1, "p")
    got("thm1", "thp1")
    to_core(2, 1)
    got("iym11", "iyp10")
    s_tile(0, 5, 7, 0, 2)
    s_tile(0, 5, 7, 2, 4)
    s_tile(1, 5, 7, 0, 3)
    got("tc21")
    s_tile(1, 0, 4, 3, 4)
    s_tile(1, 4, 7, 3, 4)
    got("ihm1", "ihp1")
    s_tile(0, 7, 8, 0, 4)
    s_tile(1, 7, 8, 0, 4)

    for a in range(2):
        m = mc[a]
        top = jnp.max(m, axis=0, keepdims=True)
        total = jnp.sum(sc[a] * jnp.exp2(m - top), axis=0, keepdims=True)
        LC[0, a : a + 1, :] = top + jnp.log(total) * LOG2E
    for q, (r, a, b) in inner_peers:
        send(f"lc{q}", LC.at[0], LC.at[INNER.index((-r % 4, a, b))], at(dz=r, dl=a, dc=b))
    for s in range(8):
        m = mr[s].T
        top = jnp.max(m, axis=0, keepdims=True)
        total = jnp.sum(sr[s].T * jnp.exp2(m - top), axis=0, keepdims=True)
        LR[0, s : s + 1, :] = top + jnp.log(total) * LOG2E
    for s, (a, r) in outer_peers:
        send(f"lr{s}", LR.at[0], LR.at[SLOT[a, -r % 4]], at(dh=a, dy=r))

    def merge(parts):
        top = functools.reduce(jnp.maximum, parts)
        total = functools.reduce(jnp.add, [jnp.exp2(part - top) for part in parts])
        return top + jnp.log(total) * LOG2E

    got(*[f"lc{q}" for q, _ in inner_peers])
    col_own = None
    for a in range(2):
        for g, r in enumerate(Z_OFF):
            parts = []
            for q, (dr, da, _) in enumerate(INNER):
                there = GROUP[(r - dr) % 4]
                parts.append(LC[q, (a ^ da) : (a ^ da) + 1, there * Q : (there + 1) * Q])
            lse = merge(parts)
            if a == 0 and g == 0:
                col_own = lse
            lcol[a, :, g * Q : (g + 1) * Q] = jnp.broadcast_to(lse + 1.0, (8, Q))
    got(*[f"lr{s}" for s, _ in outer_peers])
    row_own = None
    for s, (a, r) in enumerate(SLOTS):
        parts = []
        for p, (da, dr) in enumerate(SLOTS):
            there = SLOT[a ^ da, (r - dr) % 4]
            parts.append(LR[p, there : there + 1, :])
        lse = merge(parts)
        if s == 0:
            row_own = lse
        mr[s] = jnp.broadcast_to(lse + 1.0, (128, RP)).T

    def w_unit(a, first, last, slot):
        rows = pl.ds(pl.multiple_of(slot * R, R), R)
        by_row = mr[slot, 0:R, :]
        for j in range(first * Q, last * Q, 128):
            cols = slice(j, j + 128)
            s = S[a, rows, cols]
            w = jnp.exp2(s - by_row) + jnp.exp2(s - lcol[a, 0:1, cols])
            W[a, rows, cols] = w.astype(jnp.bfloat16)

    done = set()

    def w_need(a, first, last, slots):
        todo = [s for s in slots if (a, first, s) not in done]
        done.update((a, g, s) for g in range(first, last) for s in todo)
        while todo:
            lo = hi = todo.pop(0)
            while todo and todo[0] == hi + 1:
                hi = todo.pop(0)
            lax.fori_loop(lo, hi + 1, lambda slot, _: (w_unit(a, first, last, slot), 0)[1], 0)

    def t_terms(a, g):
        w_need(a, g, g + 1, range(8))
        if a == 0:
            started[f"cs1{g}"].wait_send()
        PT[g] = dot_tn(W[a, :, g * Q : (g + 1) * Q], I[...])
        send(f"cs{a}{g}", PT.at[g, pl.ds(core_row(1), R), :], CR.at[a, g], at(dc=1))

    def t_sum(a, g, h):
        rows = pl.ds(pl.multiple_of(core_row(0) + h * H, H), H)
        return PT[g, rows, :] + CR[a, g, h * H : (h + 1) * H, :]

    def i_terms(slot):
        for a in range(2):
            for g in range(4):
                w_need(a, g, g + 1, [slot])
        rows = slice(slot * R, (slot + 1) * R)
        return dot_nn(W[0, rows, :], T[0]) + dot_nn(W[1, rows, :], T[1])

    def far_t(a):
        got(f"cs{a}3")
        for i, d in enumerate("mp"):
            ZS[a, 0, i] = t_sum(a, 3, i).astype(jnp.bfloat16)
            send(f"zh{d}{a}", ZS.at[a, 0, i], ZH.at[a, i], at(dz=1 if d == "m" else 3))

    def far_i(a):
        term = i_terms(SLOT[a, 2])
        for i, d in enumerate("mp"):
            YS[a, 0, i] = term[i * H : (i + 1) * H].astype(jnp.bfloat16)
            send(f"yh{d}{a}", YS.at[a, 0, i], YH.at[a, i], at(dy=1 if d == "m" else 3))

    def near_t(a, d):
        i = "mp".index(d)
        g = GROUP[1 if d == "m" else 3]
        got(f"cs{a}{g}")
        for h in (1 - i, i):
            part = t_sum(a, g, h)
            if h == i:
                got(f"zh{d}{a}")
                part = part + ZH[a, i].astype(jnp.float32)
            ZS[a, 1 + i, h] = part.astype(jnp.bfloat16)
            send(f"zn{d}{a}{h}", ZS.at[a, 1 + i, h], ZN.at[a, i, h], at(dz=1 if d == "m" else 3))

    def near_i(a, d):
        i = "mp".index(d)
        term = i_terms(SLOT[a, 1 if d == "m" else 3])
        for h in (1 - i, i):
            part = term[h * H : (h + 1) * H]
            if h == i:
                got(f"yh{d}{a}")
                part = part + YH[a, i].astype(jnp.float32)
            YS[a, 1 + i, h] = part.astype(jnp.bfloat16)
            send(f"yn{d}{a}{h}", YS.at[a, 1 + i, h], YN.at[a, i, h], at(dy=1 if d == "m" else 3))

    def ring_sum(name, held, a, h, term):
        got(f"{name}m{a}{h}", f"{name}p{a}{h}")
        return term + (held[a, 0, h].astype(jnp.float32) + held[a, 1, h].astype(jnp.float32))

    t_terms(1, 3)
    far_i(1)
    t_terms(1, 1)
    far_t(1)
    t_terms(1, 2)
    near_t(1, "m")
    near_i(1, "m")
    near_t(1, "p")
    near_i(1, "p")
    t_terms(1, 0)
    ig_ref[...] = i_terms(SLOT[1, 0])
    got("cs10")
    for h in range(2):
        rows = slice(h * H, (h + 1) * H)
        tg_ref[rows, :] = t_sum(1, 0, h)
    t_terms(0, 3)
    far_i(0)
    t_terms(0, 1)
    far_t(0)
    for h in range(2):
        rows = slice(h * H, (h + 1) * H)
        XS[0, rows, :] = ring_sum("zn", ZN, 1, h, tg_ref[rows, :]).astype(jnp.bfloat16)
        send(f"xs{h}", XS.at[0, rows, :], XR.at[0, rows, :], at(dl=1))
    t_terms(0, 2)
    near_t(0, "m")
    near_i(0, "m")
    for h in range(2):
        rows = slice(h * H, (h + 1) * H)
        XS[1, rows, :] = ring_sum("yn", YN, 1, h, ig_ref[rows, :]).astype(jnp.bfloat16)
        send(f"xi{h}", XS.at[1, rows, :], XR.at[1, rows, :], at(dh=1))
    near_t(0, "p")
    near_i(0, "p")

    col_mine = jnp.where(c == 0, col_own[:, 0:R], col_own[:, R:Q])
    diag_own = jnp.sum(dsum[...].T, axis=0, keepdims=True)[:, 0:R] * k2
    LO[0] = jnp.full((8, 128), jnp.sum(row_own[:, 0:R] + col_mine - 2.0 * diag_own), jnp.float32)
    for s, (a, r) in outer_peers:
        send(f"lo{s}", LO.at[0], LO.at[SLOT[a, -r % 4]], at(dh=a, dy=r))

    t_terms(0, 0)

    def ring(values):
        return (values[0] + values[2]) + (values[1] + values[3])

    got(*[f"lo{s}" for s, _ in outer_peers])
    LI[0] = ring([LO[SLOT[0, r]] for r in range(4)]) + ring([LO[SLOT[1, r]] for r in range(4)])
    for q, (r, a, b) in inner_peers:
        send(f"li{q}", LI.at[0], LI.at[INNER.index((-r % 4, a, b))], at(dz=r, dl=a, dc=b))

    ig_ref[...] = i_terms(SLOT[0, 0])
    got("cs00")
    for h in range(2):
        rows = slice(h * H, (h + 1) * H)
        tg_ref[rows, :] = ring_sum("zn", ZN, 0, h, t_sum(0, 0, h)) - I[rows, :].astype(jnp.float32)
        text = T[0, trows(0, 0, h), :].astype(jnp.float32)
        ig_ref[rows, :] = ring_sum("yn", YN, 0, h, ig_ref[rows, :]) - text

    got(*[f"li{q}" for q, _ in inner_peers])
    by_z = []
    for r in range(4):
        v = [[LI[INNER.index((r, a, b))] for b in range(2)] for a in range(2)]
        by_z.append((v[0][0] + v[0][1]) + (v[1][0] + v[1][1]))
    loss_ref[...] = (ring(by_z) * (LN2 / (2 * 128 * R)))[0:1, 0:1]

    for h in range(2):
        rows = slice(h * H, (h + 1) * H)
        got(f"xs{h}")
        tg_ref[rows, :] = k * (tg_ref[rows, :] + XR[0, rows, :].astype(jnp.float32))
        got(f"xi{h}")
        ig_ref[rows, :] = k * (ig_ref[rows, :] + XR[1, rows, :].astype(jnp.float32))
    for name in started:
        if not name.startswith("cs1"):
            started[name].wait_send()


def per_device(image_codes, image_exps, text_codes, text_exps, logit_scale):
    R, D = image_codes.shape
    H = R // 2
    C = 8 * R
    RP = -(-R // 128) * 128
    bf16, f32 = jnp.bfloat16, jnp.float32
    vmem = pl.BlockSpec(memory_space=pltpu.VMEM)
    scratch = [
        pltpu.VMEM((2, C, D), bf16),
        pltpu.VMEM((C, D), bf16),
        pltpu.VMEM((2, C, C), f32),
        pltpu.VMEM((2, C, C), bf16),
        pltpu.VMEM((8, RP, 128), f32),
        pltpu.VMEM((8, RP, 128), f32),
        pltpu.VMEM((2, 8, C), f32),
        pltpu.VMEM((2, 8, C), f32),
        pltpu.VMEM((2, 8, C), f32),
        pltpu.VMEM((8, 8, RP), f32),
        pltpu.VMEM((16, 2, C), f32),
        pltpu.VMEM((8, 8, 128), f32),
        pltpu.VMEM((16, 8, 128), f32),
        pltpu.VMEM((4, 2 * R, D), f32),
        pltpu.VMEM((2, 4, R, D), f32),
        pltpu.VMEM((2, 3, 2, H, D), bf16),
        pltpu.VMEM((2, 2, H, D), bf16),
        pltpu.VMEM((2, 2, 2, H, D), bf16),
        pltpu.VMEM((2, 3, 2, H, D), bf16),
        pltpu.VMEM((2, 2, H, D), bf16),
        pltpu.VMEM((2, 2, 2, H, D), bf16),
        pltpu.VMEM((2, R, D), bf16),
        pltpu.VMEM((2, R, D), bf16),
        pltpu.VMEM((RP, 128), f32),
        pltpu.VMEM((128, RP), jnp.int32),
        pltpu.SemaphoreType.DMA((len(MESSAGES),)),
        pltpu.SemaphoreType.DMA((len(MESSAGES),)),
    ]
    loss, image_grad, text_grad = pl.pallas_call(
        kernel,
        out_shape=[
            jax.ShapeDtypeStruct((1, 1), f32),
            jax.ShapeDtypeStruct((R, D), f32),
            jax.ShapeDtypeStruct((R, D), f32),
        ],
        in_specs=[vmem, vmem, vmem, vmem, pl.BlockSpec(memory_space=pltpu.SMEM)],
        out_specs=[vmem, vmem, vmem],
        scratch_shapes=scratch,
        compiler_params=pltpu.CompilerParams(
            collective_id=0, has_side_effects=True, vmem_limit_bytes=63 * 1024 * 1024
        ),
    )(image_codes, image_exps.T, text_codes, text_exps.T, logit_scale)
    return loss.reshape(()), image_grad, text_grad


def solution(mesh):
    rows = P(("outer", "inner"), None)
    return jax.shard_map(
        per_device, mesh=mesh, in_specs=(rows, rows, rows, rows, P()), out_specs=(P(), rows, rows), check_vma=False
    )
```

time: 111 us -> 99.7 us (0.90)
  Pallas kernels: 104 us -> 93.7 us
  local copies, waits for them, and re-layouts: 6.23 us -> 2.8 us
  between operations: 1.3 us -> 3.03 us
    pallas_call x1, Pallas kernels: 104 us -> 93.7 us  [per_device(): pl.pallas_call(kernel, out_shape=[jax.ShapeDtypeStruct((1, 1), f32), jax....]
    unnamed x8 -> x4, local copies, waits for them, and re-layouts: 5.03 us -> 2.8 us
    slice x1 -> x0, local copies, waits for them, and re-layouts: 1.19 us -> none  [per_device(): return (loss[0, 0], image_grad, text_grad)]
where the time goes in v2:
time: 99.7 us; the launch traced here: 99.6 us
  Pallas kernels  93.7 us (94%)
  between operations  3.03 us (3%)
  local copies, waits for them, and re-layouts  2.8 us (3%)
    pallas_call x1, Pallas kernels, per_device(): pl.pallas_call(kernel, out_shape=[jax.ShapeDtypeStruct((1, 1), f32), jax....  93.7 us
    unnamed x4, local copies, waits for them, and re-layouts  2.8 us

profile of v2, /device:TPU:1, one launch (start us, length us, event | category | flops | bytes accessed | tf_op | source)
XLA Modules:
  0.0 99.6 jit_solution(2381008793930036929)
XLA Ops:
  1.3 93.7 %shard_map.76 = (f32[1,1]{1,0:T(1,128)}, f32[192,768]{1,0:T(8,128)}, f32[192,768]{1,0:T(8,128)}) custom-call(s32[192,768]{1,0:T(8,128)} %ic_ref.1, s32[6,192]{1,0:T(8,128)} %bitcast.3, s32[192,768]{1,0:T(8,128)} %tc_ref.1, s32[6,192]{1,0:T(8,128)} %bitcast.4, f32[1]{0:T(128)S(6)} %copy.11.scale_ref), custom_call_target="tpu_custom_call" | custom-call | tf_op jit(solution)/shard_map/pallas_call | solution.py:483
  95.6 0.0 copy-start
  95.6 2.0 %copy.13 = f32[192,768]{1,0:T(8,128)} copy(f32[192,768]{1,0:T(8,128)} %get-tuple-element.13) | data formatting | bytes 1179648
  97.6 0.0 copy-done
  97.6 0.8 copy.14
Async XLA Ops:
  95.6 2.0 %copy-start = (f32[192,768]{1,0:T(8,128)S(1)}, f32[192,768]{1,0:T(8,128)}, u32[]{:S(2)}) copy-start(f32[192,768]{1,0:T(8,128)} %get-tuple-element.14) | copy-start | bytes 1769476

commit v3 on v2

--- a/solution.py
+++ b/solution.py
@@ -44,7 +44,7 @@
 def kernel(
     ic_ref, ie_ref, tc_ref, te_ref, scale_ref, loss_ref, ig_ref, tg_ref,
     T, I, S, W, mr, sr, mc, sc, lcol, LR, LC, LO, LI,
-    PT, CR, ZS, ZH, ZN, YS, YH, YN, XS, XR, dsum, exps, send_sems, recv_sems,
+    PT, CR, ZS, ZH, ZN, YS, YH, YN, KI, XS, XR, dsum, exps, send_sems, recv_sems,
 ):
     R, D = ic_ref.shape
     H = R // 2
@@ -244,10 +244,17 @@
     got("tc21")
     s_tile(1, 0, 4, 3, 4)
     s_tile(1, 4, 7, 3, 4)
+    def row_lse(s):
+        m = mr[s].T
+        top = jnp.max(m, axis=0, keepdims=True)
+        total = jnp.sum(sr[s].T * jnp.exp2(m - top), axis=0, keepdims=True)
+        LR[0, s : s + 1, :] = top + jnp.log(total) * LOG2E
+
+    for s in range(7):
+        row_lse(s)
     got("ihm1", "ihp1")
     s_tile(0, 7, 8, 0, 4)
     s_tile(1, 7, 8, 0, 4)
-
     for a in range(2):
         m = mc[a]
         top = jnp.max(m, axis=0, keepdims=True)
@@ -255,11 +262,7 @@
         LC[0, a : a + 1, :] = top + jnp.log(total) * LOG2E
     for q, (r, a, b) in inner_peers:
         send(f"lc{q}", LC.at[0], LC.at[INNER.index((-r % 4, a, b))], at(dz=r, dl=a, dc=b))
-    for s in range(8):
-        m = mr[s].T
-        top = jnp.max(m, axis=0, keepdims=True)
-        total = jnp.sum(sr[s].T * jnp.exp2(m - top), axis=0, keepdims=True)
-        LR[0, s : s + 1, :] = top + jnp.log(total) * LOG2E
+    row_lse(7)
     for s, (a, r) in outer_peers:
         send(f"lr{s}", LR.at[0], LR.at[SLOT[a, -r % 4]], at(dh=a, dy=r))
 
@@ -292,10 +295,16 @@
             row_own = lse
         mr[s] = jnp.broadcast_to(lse + 1.0, (128, RP)).T
 
-    def w_unit(a, first, last, slot):
-        rows = pl.ds(pl.multiple_of(slot * R, R), R)
+    col_mine = jnp.where(c == 0, col_own[:, 0:R], col_own[:, R:Q])
+    diag_own = jnp.sum(dsum[...].T, axis=0, keepdims=True)[:, 0:R] * k2
+    LO[0] = jnp.full((1, 128), jnp.sum(row_own[:, 0:R] + col_mine - 2.0 * diag_own), jnp.float32)
+    for s, (a, r) in outer_peers:
+        send(f"lo{s}", LO.at[0], LO.at[SLOT[a, -r % 4]], at(dh=a, dy=r))
+
+    def w_unit(a, g, slot):
+        rows = slice(slot * R, (slot + 1) * R)
         by_row = mr[slot, 0:R, :]
-        for j in range(first * Q, last * Q, 128):
+        for j in range(g * Q, (g + 1) * Q, 128):
             cols = slice(j, j + 128)
             s = S[a, rows, cols]
             w = jnp.exp2(s - by_row) + jnp.exp2(s - lcol[a, 0:1, cols])
@@ -303,19 +312,23 @@
 
     done = set()
 
-    def w_need(a, first, last, slots):
-        todo = [s for s in slots if (a, first, s) not in done]
-        done.update((a, g, s) for g in range(first, last) for s in todo)
-        while todo:
-            lo = hi = todo.pop(0)
-            while todo and todo[0] == hi + 1:
-                hi = todo.pop(0)
-            lax.fori_loop(lo, hi + 1, lambda slot, _: (w_unit(a, first, last, slot), 0)[1], 0)
-
-    def t_terms(a, g):
-        w_need(a, g, g + 1, range(8))
+    def weights(needed):
+        for unit in needed:
+            if unit not in done:
+                done.add(unit)
+                w_unit(*unit)
+
+    def for_t(a, g):
+        return [(a, g, slot) for slot in range(8)]
+
+    def for_i(slot):
+        return [(a, g, slot) for a in range(2) for g in range(4)]
+
+    def t_terms(a, g, then=()):
+        weights(for_t(a, g))
         if a == 0:
             started[f"cs1{g}"].wait_send()
+        weights(then)
         PT[g] = dot_tn(W[a, :, g * Q : (g + 1) * Q], I[...])
         send(f"cs{a}{g}", PT.at[g, pl.ds(core_row(1), R), :], CR.at[a, g], at(dc=1))
 
@@ -323,10 +336,9 @@
         rows = pl.ds(pl.multiple_of(core_row(0) + h * H, H), H)
         return PT[g, rows, :] + CR[a, g, h * H : (h + 1) * H, :]
 
-    def i_terms(slot):
-        for a in range(2):
-            for g in range(4):
-                w_need(a, g, g + 1, [slot])
+    def i_terms(slot, then=()):
+        weights(for_i(slot))
+        weights(then)
         rows = slice(slot * R, (slot + 1) * R)
         return dot_nn(W[0, rows, :], T[0]) + dot_nn(W[1, rows, :], T[1])
 
@@ -336,79 +348,53 @@
             ZS[a, 0, i] = t_sum(a, 3, i).astype(jnp.bfloat16)
             send(f"zh{d}{a}", ZS.at[a, 0, i], ZH.at[a, i], at(dz=1 if d == "m" else 3))
 
-    def far_i(a):
-        term = i_terms(SLOT[a, 2])
+    def far_i(a, then):
+        term = i_terms(SLOT[a, 2], then)
         for i, d in enumerate("mp"):
             YS[a, 0, i] = term[i * H : (i + 1) * H].astype(jnp.bfloat16)
             send(f"yh{d}{a}", YS.at[a, 0, i], YH.at[a, i], at(dy=1 if d == "m" else 3))
 
-    def near_t(a, d):
-        i = "mp".index(d)
-        g = GROUP[1 if d == "m" else 3]
-        got(f"cs{a}{g}")
-        for h in (1 - i, i):
-            part = t_sum(a, g, h)
-            if h == i:
-                got(f"zh{d}{a}")
-                part = part + ZH[a, i].astype(jnp.float32)
-            ZS[a, 1 + i, h] = part.astype(jnp.bfloat16)
-            send(f"zn{d}{a}{h}", ZS.at[a, 1 + i, h], ZN.at[a, i, h], at(dz=1 if d == "m" else 3))
-
-    def near_i(a, d):
-        i = "mp".index(d)
-        term = i_terms(SLOT[a, 1 if d == "m" else 3])
-        for h in (1 - i, i):
-            part = term[h * H : (h + 1) * H]
-            if h == i:
-                got(f"yh{d}{a}")
-                part = part + YH[a, i].astype(jnp.float32)
-            YS[a, 1 + i, h] = part.astype(jnp.bfloat16)
-            send(f"yn{d}{a}{h}", YS.at[a, 1 + i, h], YN.at[a, i, h], at(dy=1 if d == "m" else 3))
+    def z_send(a, i, h, part):
+        ZS[a, 1 + i, h] = part.astype(jnp.bfloat16)
+        send(f"zn{'mp'[i]}{a}{h}", ZS.at[a, 1 + i, h], ZN.at[a, i, h], at(dz=3 if i else 1))
+
+    def y_send(a, i, h, part):
+        YS[a, 1 + i, h] = part.astype(jnp.bfloat16)
+        send(f"yn{'mp'[i]}{a}{h}", YS.at[a, 1 + i, h], YN.at[a, i, h], at(dy=3 if i else 1))
+
+    def near_t(a, i):
+        g = GROUP[3 if i else 1]
+        if (a, i) != (1, 1):
+            got(f"cs{a}{g}")
+        z_send(a, i, 1 - i, t_sum(a, g, 1 - i))
+
+    def near_t_met(a, i):
+        g = GROUP[3 if i else 1]
+        if (a, i) == (1, 1):
+            got(f"cs{a}{g}")
+        got(f"zh{'mp'[i]}{a}")
+        z_send(a, i, i, t_sum(a, g, i) + ZH[a, i].astype(jnp.float32))
+
+    def near_i(a, i, then):
+        term = i_terms(SLOT[a, 3 if i else 1], then)
+        y_send(a, i, 1 - i, term[(1 - i) * H : (2 - i) * H])
+        KI[i] = term[i * H : (i + 1) * H]
+
+    def near_i_met(a, i):
+        got(f"yh{'mp'[i]}{a}")
+        y_send(a, i, i, KI[i] + YH[a, i].astype(jnp.float32))
 
     def ring_sum(name, held, a, h, term):
         got(f"{name}m{a}{h}", f"{name}p{a}{h}")
         return term + (held[a, 0, h].astype(jnp.float32) + held[a, 1, h].astype(jnp.float32))
 
-    t_terms(1, 3)
-    far_i(1)
-    t_terms(1, 1)
+    halves = [(h, slice(h * H, (h + 1) * H)) for h in range(2)]
+    t_terms(1, 3, for_t(1, 1))
+    t_terms(1, 1, for_t(1, 2))
     far_t(1)
-    t_terms(1, 2)
-    near_t(1, "m")
-    near_i(1, "m")
-    near_t(1, "p")
-    near_i(1, "p")
-    t_terms(1, 0)
-    ig_ref[...] = i_terms(SLOT[1, 0])
-    got("cs10")
-    for h in range(2):
-        rows = slice(h * H, (h + 1) * H)
-        tg_ref[rows, :] = t_sum(1, 0, h)
-    t_terms(0, 3)
-    far_i(0)
-    t_terms(0, 1)
-    far_t(0)
-    for h in range(2):
-        rows = slice(h * H, (h + 1) * H)
-        XS[0, rows, :] = ring_sum("zn", ZN, 1, h, tg_ref[rows, :]).astype(jnp.bfloat16)
-        send(f"xs{h}", XS.at[0, rows, :], XR.at[0, rows, :], at(dl=1))
-    t_terms(0, 2)
-    near_t(0, "m")
-    near_i(0, "m")
-    for h in range(2):
-        rows = slice(h * H, (h + 1) * H)
-        XS[1, rows, :] = ring_sum("yn", YN, 1, h, ig_ref[rows, :]).astype(jnp.bfloat16)
-        send(f"xi{h}", XS.at[1, rows, :], XR.at[1, rows, :], at(dh=1))
-    near_t(0, "p")
-    near_i(0, "p")
-
-    col_mine = jnp.where(c == 0, col_own[:, 0:R], col_own[:, R:Q])
-    diag_own = jnp.sum(dsum[...].T, axis=0, keepdims=True)[:, 0:R] * k2
-    LO[0] = jnp.full((8, 128), jnp.sum(row_own[:, 0:R] + col_mine - 2.0 * diag_own), jnp.float32)
-    for s, (a, r) in outer_peers:
-        send(f"lo{s}", LO.at[0], LO.at[SLOT[a, -r % 4]], at(dh=a, dy=r))
-
-    t_terms(0, 0)
+    t_terms(1, 2, for_i(SLOT[1, 2]))
+    near_t(1, 0)
+    far_i(1, for_t(1, 0))
 
     def ring(values):
         return (values[0] + values[2]) + (values[1] + values[3])
@@ -418,11 +404,50 @@
     for q, (r, a, b) in inner_peers:
         send(f"li{q}", LI.at[0], LI.at[INNER.index((-r % 4, a, b))], at(dz=r, dl=a, dc=b))
 
+    t_terms(1, 0, for_i(SLOT[1, 1]))
+    near_t_met(1, 1)
+    near_t(1, 1)
+    near_t_met(1, 0)
+    near_i(1, 0, for_i(SLOT[1, 3]))
+    near_i(1, 1, for_i(SLOT[1, 0]))
+    near_i_met(1, 0)
+    near_i_met(1, 1)
+    ig_ref[...] = i_terms(SLOT[1, 0], for_t(0, 3))
+    t_terms(0, 3, for_t(0, 1))
+
+    def across_t(h):
+        rows = halves[h][1]
+        XS[0, rows, :] = ring_sum("zn", ZN, 1, h, t_sum(1, 0, h)).astype(jnp.bfloat16)
+        send(f"xs{h}", XS.at[0, rows, :], XR.at[0, rows, :], at(dl=1))
+
+    def across_i(h):
+        rows = halves[h][1]
+        XS[1, rows, :] = ring_sum("yn", YN, 1, h, ig_ref[rows, :]).astype(jnp.bfloat16)
+        send(f"xi{h}", XS.at[1, rows, :], XR.at[1, rows, :], at(dh=1))
+
+    got("cs10")
+    across_t(1)
+    t_terms(0, 1, for_t(0, 2))
+    far_t(0)
+    t_terms(0, 2, for_i(SLOT[0, 2]))
+    across_t(0)
+    far_i(0, for_i(SLOT[0, 1]))
+    near_t(0, 0)
+    near_t(0, 1)
+    across_i(0)
+    across_i(1)
+    near_i(0, 0, for_i(SLOT[0, 3]))
+    near_i(0, 1, for_t(0, 0))
+    near_t_met(0, 0)
+    near_t_met(0, 1)
+    near_i_met(0, 0)
+    near_i_met(0, 1)
+    t_terms(0, 0, for_i(SLOT[0, 0]))
     ig_ref[...] = i_terms(SLOT[0, 0])
     got("cs00")
-    for h in range(2):
-        rows = slice(h * H, (h + 1) * H)
+    for h, rows in halves:
         tg_ref[rows, :] = ring_sum("zn", ZN, 0, h, t_sum(0, 0, h)) - I[rows, :].astype(jnp.float32)
+    for h, rows in halves:
         text = T[0, trows(0, 0, h), :].astype(jnp.float32)
         ig_ref[rows, :] = ring_sum("yn", YN, 0, h, ig_ref[rows, :]) - text
 
@@ -463,8 +488,8 @@
         pltpu.VMEM((2, 8, C), f32),
         pltpu.VMEM((8, 8, RP), f32),
         pltpu.VMEM((16, 2, C), f32),
-        pltpu.VMEM((8, 8, 128), f32),
-        pltpu.VMEM((16, 8, 128), f32),
+        pltpu.VMEM((8, 1, 128), f32),
+        pltpu.VMEM((16, 1, 128), f32),
         pltpu.VMEM((4, 2 * R, D), f32),
         pltpu.VMEM((2, 4, R, D), f32),
         pltpu.VMEM((2, 3, 2, H, D), bf16),
@@ -473,6 +498,7 @@
         pltpu.VMEM((2, 3, 2, H, D), bf16),
         pltpu.VMEM((2, 2, H, D), bf16),
         pltpu.VMEM((2, 2, 2, H, D), bf16),
+        pltpu.VMEM((2, H, D), f32),
         pltpu.VMEM((2, R, D), bf16),
         pltpu.VMEM((2, R, D), bf16),
         pltpu.VMEM((RP, 128), f32),

time: 99.7 us -> 89.1 us (0.89)
  Pallas kernels: 93.7 us -> 83.1 us
    pallas_call x1, Pallas kernels: 93.7 us -> 83.1 us  [per_device(): pl.pallas_call(kernel, out_shape=[jax.ShapeDtypeStruct((1, 1), f32), jax....]
where the time goes in v3:
time: 89.1 us; the launch traced here: 88.9 us
  Pallas kernels  83.1 us (93%)
  between operations  3.03 us (3%)
  local copies, waits for them, and re-layouts  2.8 us (3%)
    pallas_call x1, Pallas kernels, per_device(): pl.pallas_call(kernel, out_shape=[jax.ShapeDtypeStruct((1, 1), f32), jax....  83.1 us
    unnamed x4, local copies, waits for them, and re-layouts  2.8 us

profile of v3, /device:TPU:1, one launch (start us, length us, event | category | flops | bytes accessed | tf_op | source)
XLA Modules:
  0.0 88.9 jit_solution(3155226788317535617)
XLA Ops:
  1.3 83.1 %shard_map.76 = (f32[1,1]{1,0:T(1,128)}, f32[192,768]{1,0:T(8,128)}, f32[192,768]{1,0:T(8,128)}) custom-call(s32[192,768]{1,0:T(8,128)} %ic_ref.1, s32[6,192]{1,0:T(8,128)} %bitcast.3, s32[192,768]{1,0:T(8,128)} %tc_ref.1, s32[6,192]{1,0:T(8,128)} %bitcast.4, f32[1]{0:T(128)S(6)} %copy.11.scale_ref), custom_call_target="tpu_custom_call" | custom-call | tf_op jit(solution)/shard_map/pallas_call | solution.py:509
  85.0 0.0 copy-start
  85.0 2.0 %copy.13 = f32[192,768]{1,0:T(8,128)} copy(f32[192,768]{1,0:T(8,128)} %get-tuple-element.13) | data formatting | bytes 1179648
  87.0 0.0 copy-done
  87.0 0.8 copy.14
Async XLA Ops:
  85.0 2.0 %copy-start = (f32[192,768]{1,0:T(8,128)S(1)}, f32[192,768]{1,0:T(8,128)}, u32[]{:S(2)}) copy-start(f32[192,768]{1,0:T(8,128)} %get-tuple-element.14) | copy-start | bytes 1769476

commit v4 on v3

--- a/solution.py
+++ b/solution.py
@@ -42,11 +42,13 @@
 
 
 def kernel(
-    ic_ref, ie_ref, tc_ref, te_ref, scale_ref, loss_ref, ig_ref, tg_ref,
+    ic_hbm, ie_ref, tc_hbm, te_ref, scale_ref, loss_ref, ig_hbm, tg_hbm,
     T, I, S, W, mr, sr, mc, sc, lcol, LR, LC, LO, LI,
-    PT, CR, ZS, ZH, ZN, YS, YH, YN, KI, XS, XR, dsum, exps, send_sems, recv_sems,
+    PT, CR, ZS, ZH, ZN, YS, YH, YN, KI, XS, XR, dsum, exps, codes, grads, own_sems, send_sems, recv_sems,
 ):
-    R, D = ic_ref.shape
+    R, D = ic_hbm.shape
+    ic_ref, tc_ref = codes.at[0], codes.at[1]
+    ig_ref, tg_ref = grads.at[0], grads.at[1]
     H = R // 2
     Q = 2 * R
     C = 8 * R
@@ -72,6 +74,10 @@
         pl.semaphore_signal(barrier, inc=1, device_id=at(dh=a, dy=r), device_id_type=MESH)
     for _, (r, a, b) in inner_peers:
         pl.semaphore_signal(barrier, inc=1, device_id=at(dz=r, dl=a, dc=b), device_id_type=MESH)
+    text_in = pltpu.make_async_copy(tc_hbm, tc_ref, own_sems.at[0])
+    image_in = pltpu.make_async_copy(ic_hbm, ic_ref, own_sems.at[1])
+    text_in.start()
+    image_in.start()
 
     started = {}
 
@@ -117,12 +123,9 @@
     exps[...] = jnp.zeros(exps.shape, jnp.int32)
     image_exps = columns(ie_ref)
     text_exps = columns(te_ref)
-    diag = jnp.zeros((R, 128), jnp.float32)
+    text_in.wait()
     for f in range(ND):
-        image = decode(ic_ref, image_exps, f)
         text = decode(tc_ref, text_exps, f)
-        diag = diag + image * text
-        I[0:R, f * 128 : (f + 1) * 128] = image.astype(jnp.bfloat16)
         T[0, trows(0, 0), f * 128 : (f + 1) * 128] = text.astype(jnp.bfloat16)
 
     pl.semaphore_wait(barrier, 22)
@@ -148,19 +151,28 @@
     def to_core(r, a):
         send(f"tc{r}{a}", tpart(a, r), tpart(a, r), at(dc=1))
 
-    for d in "mp":
-        ring_t(0, d, 0 if d == "m" else 1)
-        ring_i(0, d, 0 if d == "m" else 1)
+    ring_t(0, "m", 0)
+    ring_t(0, "p", 1)
     for h in range(2):
         send(f"tx{h}", tpart(0, 0, h), tpart(1, 0, h), at(dl=1))
-    for d in "mp":
-        ring_t(0, d, 1 if d == "m" else 0)
-        ring_i(0, d, 1 if d == "m" else 0)
+    ring_t(0, "m", 1)
+    ring_t(0, "p", 0)
+    to_core(0, 0)
+    image_in.wait()
+    diag = jnp.zeros((R, 128), jnp.float32)
+    for f in range(ND):
+        image = decode(ic_ref, image_exps, f)
+        diag = diag + image * T[0, trows(0, 0), f * 128 : (f + 1) * 128].astype(jnp.float32)
+        I[0:R, f * 128 : (f + 1) * 128] = image.astype(jnp.bfloat16)
+    ring_i(0, "m", 0)
+    ring_i(0, "p", 1)
     for h in range(2):
         send(f"ix{h}", ipart(0, 0, h), ipart(1, 0, h), at(dh=1))
-    to_core(0, 0)
+    ring_i(0, "m", 1)
+    ring_i(0, "p", 0)
 
     dsum[0:R, :] = diag
+    LO[0] = jnp.zeros((1, RP), jnp.float32)
     if RP > R:
         dsum[R:RP, :] = jnp.zeros((RP - R, 128), jnp.float32)
         for s in range(8):
@@ -295,12 +307,6 @@
             row_own = lse
         mr[s] = jnp.broadcast_to(lse + 1.0, (128, RP)).T
 
-    col_mine = jnp.where(c == 0, col_own[:, 0:R], col_own[:, R:Q])
-    diag_own = jnp.sum(dsum[...].T, axis=0, keepdims=True)[:, 0:R] * k2
-    LO[0] = jnp.full((1, 128), jnp.sum(row_own[:, 0:R] + col_mine - 2.0 * diag_own), jnp.float32)
-    for s, (a, r) in outer_peers:
-        send(f"lo{s}", LO.at[0], LO.at[SLOT[a, -r % 4]], at(dh=a, dy=r))
-
     def w_unit(a, g, slot):
         rows = slice(slot * R, (slot + 1) * R)
         by_row = mr[slot, 0:R, :]
@@ -389,49 +395,56 @@
         return term + (held[a, 0, h].astype(jnp.float32) + held[a, 1, h].astype(jnp.float32))
 
     halves = [(h, slice(h * H, (h + 1) * H)) for h in range(2)]
-    t_terms(1, 3, for_t(1, 1))
-    t_terms(1, 1, for_t(1, 2))
+    t_terms(1, 3)
+    t_terms(1, 1)
     far_t(1)
     t_terms(1, 2, for_i(SLOT[1, 2]))
     near_t(1, 0)
     far_i(1, for_t(1, 0))
 
-    def ring(values):
-        return (values[0] + values[2]) + (values[1] + values[3])
-
-    got(*[f"lo{s}" for s, _ in outer_peers])
-    LI[0] = ring([LO[SLOT[0, r]] for r in range(4)]) + ring([LO[SLOT[1, r]] for r in range(4)])
-    for q, (r, a, b) in inner_peers:
-        send(f"li{q}", LI.at[0], LI.at[INNER.index((-r % 4, a, b))], at(dz=r, dl=a, dc=b))
+    col_mine = jnp.where(c == 0, col_own[:, 0:R], col_own[:, R:Q])
+    diag_own = jnp.sum(dsum[...].T, axis=0, keepdims=True) * k2
+    LO[0, :, 0:R] = row_own[:, 0:R] + col_mine - 2.0 * diag_own[:, 0:R]
+    for s, (a, r) in outer_peers:
+        send(f"lo{s}", LO.at[0], LO.at[SLOT[a, -r % 4]], at(dh=a, dy=r))
+
+
+    def across_t(h):
+        rows = halves[h][1]
+        XS[0, rows, :] = ring_sum("zn", ZN, 1, h, t_sum(1, 0, h)).astype(jnp.bfloat16)
+        send(f"xs{h}", XS.at[0, rows, :], XR.at[0, rows, :], at(dl=1))
+
+    def across_i(h):
+        rows = halves[h][1]
+        XS[1, rows, :] = ring_sum("yn", YN, 1, h, ig_ref[rows, :]).astype(jnp.bfloat16)
+        send(f"xi{h}", XS.at[1, rows, :], XR.at[1, rows, :], at(dh=1))
 
     t_terms(1, 0, for_i(SLOT[1, 1]))
     near_t_met(1, 1)
     near_t(1, 1)
     near_t_met(1, 0)
     near_i(1, 0, for_i(SLOT[1, 3]))
-    near_i(1, 1, for_i(SLOT[1, 0]))
+    near_i(1, 1, for_t(0, 3))
     near_i_met(1, 0)
     near_i_met(1, 1)
-    ig_ref[...] = i_terms(SLOT[1, 0], for_t(0, 3))
-    t_terms(0, 3, for_t(0, 1))
-
-    def across_t(h):
-        rows = halves[h][1]
-        XS[0, rows, :] = ring_sum("zn", ZN, 1, h, t_sum(1, 0, h)).astype(jnp.bfloat16)
-        send(f"xs{h}", XS.at[0, rows, :], XR.at[0, rows, :], at(dl=1))
-
-    def across_i(h):
-        rows = halves[h][1]
-        XS[1, rows, :] = ring_sum("yn", YN, 1, h, ig_ref[rows, :]).astype(jnp.bfloat16)
-        send(f"xi{h}", XS.at[1, rows, :], XR.at[1, rows, :], at(dh=1))
-
+    t_terms(0, 3, for_i(SLOT[1, 0]))
     got("cs10")
     across_t(1)
+
+    def ring(values):
+        return (values[0] + values[2]) + (values[1] + values[3])
+
+    got(*[f"lo{s}" for s, _ in outer_peers])
+    LI[0] = ring([LO[SLOT[0, r]] for r in range(4)]) + ring([LO[SLOT[1, r]] for r in range(4)])
+    for q, (r, a, b) in inner_peers:
+        send(f"li{q}", LI.at[0], LI.at[INNER.index((-r % 4, a, b))], at(dz=r, dl=a, dc=b))
+
+    ig_ref[...] = i_terms(SLOT[1, 0], for_i(SLOT[0, 2]))
+    far_t(0)
+    far_i(0, for_t(0, 1))
+    across_t(0)
     t_terms(0, 1, for_t(0, 2))
-    far_t(0)
-    t_terms(0, 2, for_i(SLOT[0, 2]))
-    across_t(0)
-    far_i(0, for_i(SLOT[0, 1]))
+    t_terms(0, 2, for_i(SLOT[0, 1]))
     near_t(0, 0)
     near_t(0, 1)
     across_i(0)
@@ -456,17 +469,32 @@
     for r in range(4):
         v = [[LI[INNER.index((r, a, b))] for b in range(2)] for a in range(2)]
         by_z.append((v[0][0] + v[0][1]) + (v[1][0] + v[1][1]))
-    loss_ref[...] = (ring(by_z) * (LN2 / (2 * 128 * R)))[0:1, 0:1]
+    loss_ref[...] = jnp.sum(ring(by_z)[:, 0:R], axis=1, keepdims=True) * (LN2 / (2 * 128 * R))
 
     for h in range(2):
         rows = slice(h * H, (h + 1) * H)
         got(f"xs{h}")
         tg_ref[rows, :] = k * (tg_ref[rows, :] + XR[0, rows, :].astype(jnp.float32))
+    text_out = pltpu.make_async_copy(tg_ref, tg_hbm, own_sems.at[2])
+    text_out.start()
+    image_out = []
+    for h in range(2):
+        rows = slice(h * H, (h + 1) * H)
         got(f"xi{h}")
         ig_ref[rows, :] = k * (ig_ref[rows, :] + XR[1, rows, :].astype(jnp.float32))
+        image_out.append(pltpu.make_async_copy(ig_ref.at[rows, :], ig_hbm.at[rows, :], own_sems.at[3 + h]))
+        image_out[h].start()
+    text_out.wait()
+    for copy in image_out:
+        copy.wait()
     for name in started:
         if not name.startswith("cs1"):
             started[name].wait_send()
+
+
+def hand_over(ig_ref, tg_ref, ig_out, tg_out):
+    ig_out[...] = ig_ref[...]
+    tg_out[...] = tg_ref[...]
 
 
 def per_device(image_codes, image_exps, text_codes, text_exps, logit_scale):
@@ -476,6 +504,7 @@
     RP = -(-R // 128) * 128
     bf16, f32 = jnp.bfloat16, jnp.float32
     vmem = pl.BlockSpec(memory_space=pltpu.VMEM)
+    hbm = pl.BlockSpec(memory_space=pl.ANY)
     scratch = [
         pltpu.VMEM((2, C, D), bf16),
         pltpu.VMEM((C, D), bf16),
@@ -488,8 +517,8 @@
         pltpu.VMEM((2, 8, C), f32),
         pltpu.VMEM((8, 8, RP), f32),
         pltpu.VMEM((16, 2, C), f32),
-        pltpu.VMEM((8, 1, 128), f32),
-        pltpu.VMEM((16, 1, 128), f32),
+        pltpu.VMEM((8, 1, RP), f32),
+        pltpu.VMEM((16, 1, RP), f32),
         pltpu.VMEM((4, 2 * R, D), f32),
         pltpu.VMEM((2, 4, R, D), f32),
         pltpu.VMEM((2, 3, 2, H, D), bf16),
@@ -503,6 +532,9 @@
         pltpu.VMEM((2, R, D), bf16),
         pltpu.VMEM((RP, 128), f32),
         pltpu.VMEM((128, RP), jnp.int32),
+        pltpu.VMEM((2, R, D), jnp.int32),
+        pltpu.VMEM((2, R, D), f32),
+        pltpu.SemaphoreType.DMA((5,)),
         pltpu.SemaphoreType.DMA((len(MESSAGES),)),
         pltpu.SemaphoreType.DMA((len(MESSAGES),)),
     ]
@@ -513,13 +545,19 @@
             jax.ShapeDtypeStruct((R, D), f32),
             jax.ShapeDtypeStruct((R, D), f32),
         ],
-        in_specs=[vmem, vmem, vmem, vmem, pl.BlockSpec(memory_space=pltpu.SMEM)],
-        out_specs=[vmem, vmem, vmem],
+        in_specs=[hbm, vmem, hbm, vmem, pl.BlockSpec(memory_space=pltpu.SMEM)],
+        out_specs=[vmem, hbm, hbm],
         scratch_shapes=scratch,
         compiler_params=pltpu.CompilerParams(
             collective_id=0, has_side_effects=True, vmem_limit_bytes=63 * 1024 * 1024
         ),
     )(image_codes, image_exps.T, text_codes, text_exps.T, logit_scale)
+    image_grad, text_grad = pl.pallas_call(
+        hand_over,
+        out_shape=[jax.ShapeDtypeStruct((R, D), f32)] * 2,
+        in_specs=[vmem] * 2,
+        out_specs=[vmem] * 2,
+    )(image_grad, text_grad)
     return loss.reshape(()), image_grad, text_grad
 
 

time: 89.1 us -> 88.6 us (level)
  local copies, waits for them, and re-layouts: 2.8 us -> 0 us
  Pallas kernels: 83.1 us -> 85.3 us
    unnamed x4 -> x0, local copies, waits for them, and re-layouts: 2.8 us -> none
    pallas_call x0 -> x1, Pallas kernels: none -> 2.29 us  [per_device(): pl.pallas_call(hand_over, out_shape=[jax.ShapeDtypeStruct((R, D), f32)] *...]
where the time goes in v4:
time: 88.6 us; the launch traced here: 88.4 us
  Pallas kernels  85.3 us (96%)
  between operations  3.02 us (3%)
    pallas_call x1, Pallas kernels, per_device(): pl.pallas_call(kernel, out_shape=[jax.ShapeDtypeStruct((1, 1), f32), jax....  83 us
    pallas_call x1, Pallas kernels, per_device(): pl.pallas_call(hand_over, out_shape=[jax.ShapeDtypeStruct((R, D), f32)] *...  2.29 us

profile of v4, /device:TPU:1, one launch (start us, length us, event | category | flops | bytes accessed | tf_op | source)
XLA Modules:
  0.0 88.4 jit_solution(6202603361362731015)
XLA Ops:
  1.3 83.0 %shard_map.76 = (f32[1,1]{1,0:T(1,128)}, f32[192,768]{1,0:T(8,128)}, f32[192,768]{1,0:T(8,128)}) custom-call(s32[192,768]{1,0:T(8,128)} %ic_hbm.1, s32[6,192]{1,0:T(8,128)} %bitcast.3, s32[192,768]{1,0:T(8,128)} %tc_hbm.1, s32[6,192]{1,0:T(8,128)} %bitcast.4, f32[1]{0:T(128)S(6)} %copy.9.scale_ref), custom_call_target="tpu_custom_call" | custom-call | tf_op jit(solution)/shard_map/pallas_call | solution.py:541
  84.3 2.3 %shard_map.77 = (f32[192,768]{1,0:T(8,128)}, f32[192,768]{1,0:T(8,128)}) custom-call(f32[192,768]{1,0:T(8,128)} %get-tuple-element.9.ig_ref, f32[192,768]{1,0:T(8,128)} %get-tuple-element.10.tg_ref), custom_call_target="tpu_custom_call" | custom-call | tf_op jit(solution)/shard_map/pallas_call | solution.py:555

commit v5 on v4

--- a/solution.py
+++ b/solution.py
@@ -245,8 +245,9 @@
     on_i(1, "m")
     s_tile(1, 4, 5, 0, 1)
     got("tc31", "tc11")
-    s_tile(1, 0, 5, 1, 3)
+    s_tile(1, 0, 5, 1, 2)
     on_i(1, "p")
+    s_tile(1, 0, 5, 2, 3)
     got("thm1", "thp1")
     to_core(2, 1)
     got("iym11", "iyp10")

time: 88.6 us -> 88.9 us (level)
  no operation moved by 1% of the time
where the time goes in v5:
time: 88.9 us; the launch traced here: 88.7 us
  Pallas kernels  85.7 us (96%)
  between operations  3.02 us (3%)
    pallas_call x1, Pallas kernels, per_device(): pl.pallas_call(kernel, out_shape=[jax.ShapeDtypeStruct((1, 1), f32), jax....  83.4 us
    pallas_call x1, Pallas kernels, per_device(): pl.pallas_call(hand_over, out_shape=[jax.ShapeDtypeStruct((R, D), f32)] *...  2.29 us

profile of v5, /device:TPU:1, one launch (start us, length us, event | category | flops | bytes accessed | tf_op | source)
XLA Modules:
  0.0 88.7 jit_solution(9195769990620544426)
XLA Ops:
  1.3 83.4 %shard_map.76 = (f32[1,1]{1,0:T(1,128)}, f32[192,768]{1,0:T(8,128)}, f32[192,768]{1,0:T(8,128)}) custom-call(s32[192,768]{1,0:T(8,128)} %ic_hbm.1, s32[6,192]{1,0:T(8,128)} %bitcast.3, s32[192,768]{1,0:T(8,128)} %tc_hbm.1, s32[6,192]{1,0:T(8,128)} %bitcast.4, f32[1]{0:T(128)S(6)} %copy.9.scale_ref), custom_call_target="tpu_custom_call" | custom-call | tf_op jit(solution)/shard_map/pallas_call | solution.py:542
  84.7 2.3 %shard_map.77 = (f32[192,768]{1,0:T(8,128)}, f32[192,768]{1,0:T(8,128)}) custom-call(f32[192,768]{1,0:T(8,128)} %get-tuple-element.9.ig_ref, f32[192,768]{1,0:T(8,128)} %get-tuple-element.10.tg_ref), custom_call_target="tpu_custom_call" | custom-call | tf_op jit(solution)/shard_map/pallas_call | solution.py:556
